TPU v7x, 256 devices: a whole 4x4x8 slice. The times are simulated.
256 devices in a mesh: gx: 8 (over x, core), gy: 16 (over z, y_lo), gz: 2 (over y_hi).
Axes of the slice: x: 4, y: 4 (y_hi: 2, y_lo: 2; y = y_hi * 2 + y_lo), z: 8, core: 2. Of those that a mesh axis runs over, the one named last changes fastest.
Arguments:
- velocity: float32 [3, 2, 4096, 4096], P(None, 'gz', 'gx', 'gy'), may hold values from -6 to 6
Outputs:
- divergence: float32 [3, 2, 4096, 4096], P(None, 'gz', 'gx', 'gy')
- coefficient: float32 [2], replicated
All inputs are finite; a program needn't handle non-finite values.
Results may differ from a plain program's by a relative error of at most 0.0003.
Values sent between devices are 32-bit elements; how exact they have to be, the bound alone decides.
No kernel may reach another device: no remote copies, remote signals or barrier semaphores. Data moves between devices by JAX's collectives and lax.ppermute only.
A program may use at most 128 MiB of HBM per device.

v0:
```python
import jax
import jax.numpy as jnp
import ml_dtypes
import numpy as np
from jax import lax
from jax.experimental import pallas as pl
from jax.experimental.pallas import tpu as pltpu
from jax.sharding import PartitionSpec as P

ROWS = 512
COLS = 256
MARGIN = 32
TILE = 128
WINDOW = TILE + 2 * MARGIN
INNER = ROWS - 2 * MARGIN
REACH = 64
POLE_F = -0.5
POLE_D = (np.sqrt(5.0) - 3.0) / 2.0
PAIRS = ((0, 0), (0, 1), (0, 2), (1, 1), (1, 2), (2, 2))
NEAR = (3, 3, 3) + (2,) * 9
FAR = (2, 2, 2) + (1,) * 9
SLOTS = tuple(n + f for n, f in zip(NEAR, FAR))
START = tuple(int(s) for s in np.concatenate(([0], np.cumsum(SLOTS)[:-1])))
SENT = sum(SLOTS)
SENT_PAD = 48
DSENT = 2
BF = jnp.bfloat16
F32 = jnp.float32


def kernels(cells=2048):
    wave = 2.0 * np.pi * np.arange(cells // 2 + 1) / cells
    filt = (0.9375 + 0.89375 * np.cos(wave) - 0.0375 * np.cos(2 * wave) + 0.00625 * np.cos(3 * wave)) / (
        1.0 + 0.8 * np.cos(wave)
    )
    deri = 1j * (14.0 / 9.0 * np.sin(wave) + np.sin(2 * wave) / 18.0) / (1.0 + 2.0 / 3.0 * np.cos(wave))
    return tuple(np.fft.irfft(s, n=cells) for s in (filt, deri, deri * filt))


KF, KD, KG = kernels()


def split(table):
    high = np.asarray(table, np.float32).astype(ml_dtypes.bfloat16)
    low = (np.asarray(table, np.float64) - high.astype(np.float64)).astype(ml_dtypes.bfloat16)
    return high, low


def toeplitz(kernel, rows, cols, shift):
    offset = np.arange(rows)[:, None] + shift - np.arange(cols)[None, :]
    return kernel[offset % len(kernel)]


def left_operand(table):
    high, low = split(table)
    return np.concatenate([high, high, low], axis=1)


def right_operand(table):
    high, low = split(table)
    return np.concatenate([high, low], axis=0)


def thrice(table, cols=slice(None)):
    half = table.shape[0] // 2
    high, low = table[:half, cols], table[half:, cols]
    return jnp.concatenate([high, high, low], axis=0)


def far_fit(kernel, poles, near):
    k = np.arange(near + 1, near + 1 + len(poles))
    weight = np.linalg.solve(np.stack([np.power(p, k) for p in poles], axis=1), kernel[k])
    k = np.arange(1, near + 1)
    rest = kernel[k] - sum(w * np.power(p, k) for w, p in zip(weight, poles))
    return weight, rest


D_FAR, D_NEAR = [float(x[0]) for x in far_fit(KD, (POLE_D,), 1)]


def from_left(kernel, poles, near, slots_near, slots_far):
    weight, rest = far_fit(kernel, poles, near)
    table = np.zeros((slots_near + slots_far, COLS))
    for m in range(1, near + 1):
        for c in range(0, near - m + 1):
            table[m - 1, c] = rest[c + m - 1]
    for s, (w, p) in enumerate(zip(weight, poles)):
        table[slots_near + s] = w * np.power(p, np.arange(COLS, dtype=np.float64))
    return table


def send_table(near, far, poles):
    depth = 64
    table = np.zeros((depth, near + far))
    for m in range(near):
        table[m, m] = 1.0
    for s in range(far):
        table[:, near + s] = np.power(poles[s], np.arange(1, depth + 1, dtype=np.float64))
    return table


def edge_table(near, far, start, width=128, second=64):
    send = send_table(near, far, (POLE_F, POLE_D) if near > 1 else (POLE_D,))
    table = np.zeros((128, width))
    n = near + far
    table[64:, start : start + n] = send[::-1]
    table[:64, second + start : second + start + n] = send
    return table


def x_tables(tile):
    f = toeplitz(KF, tile, tile + 2 * MARGIN, MARGIN)
    g = toeplitz(KG, tile, tile + 2 * MARGIN, MARGIN)
    return left_operand(np.concatenate([f, g], axis=0))


def edge_tables():
    main, rest = [], []
    for i in range(0, 12, 2):
        a, b = [edge_table(NEAR[k], FAR[k], START[k]) for k in (i, i + 1)]
        high, low = split(np.concatenate([a[:32], b[96:], b[:32], a[96:]], axis=0))
        main.append(high)
        if i < 3:
            rest.append(low)
    return np.concatenate(main + rest, axis=0)


def edge_operand(edge, fields, low):
    block = [edge[pl.ds(i * 128, 128), :] for i in range(fields + low)]
    return jnp.concatenate([b for b in block[:fields] for _ in range(2)] + block[fields:], axis=0)


ORDER = np.concatenate([np.arange(64), np.arange(192, 256), np.arange(128, 192), np.arange(64, 128)])


def y_tables():
    f = toeplitz(KF, COLS, COLS, 0).T[:, ORDER]
    g = toeplitz(KG, COLS, COLS, 0).T[:, ORDER]
    return right_operand(np.concatenate([f, g], axis=1))


def halo_tables():
    table = np.zeros((2 * SENT, 15 * 128))
    for out in range(15):
        field = out if out < 12 else out - 12
        if out < 12:
            left = from_left(KF, (POLE_F,), 2, NEAR[field], FAR[field])
            if FAR[field] == 2:
                left[NEAR[field] + 1] = 0.0
            sign = 1.0
        else:
            left = from_left(KG, (POLE_F, POLE_D), 3, NEAR[field], FAR[field])
            sign = -1.0
        left = left[:, :REACH]
        start = START[field]
        table[start : start + SLOTS[field], out * 128 : out * 128 + REACH] = left
        table[SENT + start : SENT + start + SLOTS[field], out * 128 + REACH : (out + 1) * 128] = sign * left[:, ::-1]
    full = np.zeros((256, 15 * 128), ml_dtypes.bfloat16)
    high, low = split(table)
    n = 2 * SENT
    full[:n], full[n : 2 * n], full[2 * n : 3 * n] = high, high, low
    return full


def d_edge_tables():
    main, rest = [], []
    for i in range(3):
        high, low = split(edge_table(1, 1, 2 * i, second=8))
        main.append(high)
        rest.append(low)
    return np.concatenate(main + rest, axis=0)


def d_halo_tables():
    table = np.zeros((16, 3 * 128))
    left = from_left(KD, (POLE_D,), 1, 1, 1)[:, :REACH]
    for out in range(3):
        table[2 * out : 2 * out + 2, out * 128 : out * 128 + REACH] = left
        table[8 + 2 * out : 8 + 2 * out + 2, out * 128 + REACH : (out + 1) * 128] = -left[:, ::-1]
    return right_operand(table)


def d_x_tables():
    return np.concatenate(split(toeplitz(KD, TILE, WINDOW, MARGIN)), axis=0)


def d_powers(length, sign=1.0):
    row = lax.broadcasted_iota(jnp.int32, (8, 1), 0)
    column = jnp.zeros((8, 1), F32)
    for s in range(8):
        power = POLE_D ** (s + 1) if sign > 0 else POLE_D ** (8 - s)
        column = jnp.where(row == s, float(power), column)
    blocks = range(length // 8) if sign > 0 else range(length // 8 - 1, -1, -1)
    return jnp.concatenate([column * float(POLE_D ** (8 * k)) for k in blocks], axis=0)


def d_y_tables():
    return right_operand(toeplitz(KD, COLS, COLS, 0).T[ORDER][:, ORDER])


def parts(value):
    high = value.astype(BF)
    return high, (value - high.astype(F32)).astype(BF)


def dot(a, b):
    return jnp.dot(a, b, preferred_element_type=F32)


def x_tile(window, tile, table, put, mixed, rows):
    v = [window(i) for i in range(3)]
    data = v + [v[a] * v[b] for a, b in PAIRS]
    done = [None] * 12
    for i, value in enumerate(data):
        high, low = parts(value)
        stacked = jnp.concatenate([high, low, high], axis=0)
        if i < 3:
            both = dot(table[...], stacked)
            done[i], done[3 + i] = both[:tile], both[tile:]
        else:
            done[3 + i] = dot(table[pl.ds(0, tile), :], stacked)
    lane = lax.broadcasted_iota(jnp.int32, (tile, 128), 1)
    edges = []
    for i, value in enumerate(done):
        put(i, *parts(value))
        edges.append(jnp.where(lane < 64, value[:, :128], value[:, 128:]))
    for i in range(0, 12, 2):
        both = jnp.where((lane < 32) | (lane >= 96), edges[i], pltpu.roll(edges[i + 1], 64, 1))
        high, low = parts(both)
        mixed[rows, pl.ds(128 * i, 128)] = high
        mixed[rows, pl.ds(128 * i + 128, 128)] = low
        if i < 3:
            mixed[rows, pl.ds(1536 + 64 * i, 128)] = high


def strip_kernel(first, last, first_out, last_out):
    first_out[...], last_out[...] = first[...], last[...]


def middle_kernel(v, table, small, edge, out, sent, mixed):
    at = 0
    while at < INNER:
        tile = min(TILE, INNER - at)
        rows = pl.ds(at, tile)

        def put(i, high, low):
            out[i, 0, rows, :] = high
            out[i, 1, rows, :] = low

        window = lambda i: v[i, pl.ds(at, tile + 2 * MARGIN), :]
        x_tile(window, tile, table if tile == TILE else small, put, mixed, rows)
        at += tile
    sent[...] = dot(mixed[...], edge_operand(edge, 6, 2))


def outer_kernel(v, before, after, middle, table, edge, out, to_right, to_left, mixed):
    def first(i):
        return jnp.concatenate([before[i], v[i, pl.ds(0, 2 * MARGIN), :]], axis=0)

    def last(i):
        return jnp.concatenate([v[i, pl.ds(ROWS - 2 * MARGIN, 2 * MARGIN), :], after[i]], axis=0)

    for t, window in enumerate((first, last)):
        rows = pl.ds(t * MARGIN, MARGIN)

        def put(i, high, low):
            out[i, 0, rows, :] = high
            out[i, 1, rows, :] = low

        x_tile(window, MARGIN, table, put, mixed, rows)
    sent = dot(mixed[...], edge_operand(edge, 6, 2))
    every = jnp.concatenate([sent[:MARGIN], middle[...], sent[MARGIN:]], axis=0).T
    to_right[...] = every[:SENT_PAD]
    to_left[...] = every[64 : 64 + SENT_PAD]


CHUNK = 16


def stress(f, pair_sums):
    smooth, gx, products, gy = f[0:3], f[3:6], f[6:12], f[12:15]
    sxx, syy = gx[0], gy[1]
    szz = -(sxx + syy)
    sxy = 0.5 * (gy[0] + gx[1])
    sxz = 0.5 * gx[2]
    syz = 0.5 * gy[2]
    inner = sxx * sxx + syy * syy + szz * szz + 2.0 * (sxy * sxy + sxz * sxz + syz * syz)
    magnitude = jnp.sqrt(2.0 * inner)
    strain = (sxx, sxy, sxz, syy, syz, szz)
    single, double = [
        sum((products[p] - smooth[PAIRS[p][0]] * smooth[PAIRS[p][1]]) * strain[p] for p in which)
        for which in ((0, 3, 5), (1, 2, 4))
    ]
    pair_sums[0] += (single + 2.0 * double) * magnitude
    pair_sums[1] += 2.0 * inner * inner
    return [magnitude * strain[i] for i in range(5)]


def y_kernel(middle, outer, table, out, model, pair_sums, held):
    for i in range(12):
        high, low = [
            jnp.concatenate(
                [outer[i, k, pl.ds(0, MARGIN), :], middle[i, k], outer[i, k, pl.ds(MARGIN, MARGIN), :]], axis=0
            )
            for k in range(2)
        ]
        data = jnp.concatenate([high, low, high], axis=1)
        done = dot(data, thrice(table) if i < 3 else thrice(table, slice(0, COLS)))
        out[i], held[i] = done[:, :128], done[:, 128:COLS]
        if i < 3:
            out[12 + i], held[12 + i] = done[:, COLS : COLS + 128], done[:, COLS + 128 :]
    pair_sums[...] = jnp.zeros_like(pair_sums)

    def chunk(step, carry):
        rows = pl.ds(pl.multiple_of(step * CHUNK, CHUNK), CHUNK)
        for i, value in enumerate(stress([held[k, rows, :] for k in range(15)], pair_sums)):
            model[i, rows, :] = value
        return carry

    lax.fori_loop(0, ROWS // CHUNK, chunk, 0, unroll=4)


def model_kernel(
    local, inside, inside_sums, left, right, table, edge, model, first, last, to_right, to_left, sums, halo, added, total
):
    high, low = parts(left[...])
    high2, low2 = parts(right[...])
    n = SENT
    halo[...] = jnp.zeros_like(halo)
    for k, (a, b) in enumerate(((high, high2), (low, low2), (high, high2))):
        halo[pl.ds(2 * n * k, n), :] = a.astype(F32)[:n]
        halo[pl.ds(2 * n * k + n, n), :] = b.astype(F32)[:n]
    total[...] = inside_sums[...]
    added[...] = dot(halo[...].T.astype(BF), table[...])

    def chunk(step, carry):
        rows = pl.ds(pl.multiple_of(step * CHUNK, CHUNK), CHUNK)
        f = [local[i, rows, :] + added[rows, pl.ds(i * 128, 128)] for i in range(15)]
        for i, value in enumerate(stress(f, total)):
            model[i, rows, :] = value
        return carry

    lax.fori_loop(0, ROWS // CHUNK, chunk, 0, unroll=4)
    main, rest = [], []
    for i in (1, 3, 4):
        high, low = parts(model[i])
        main += [high, low]
        rest.append(high)
    sent = dot(jnp.concatenate(main + rest, axis=1), edge_operand(edge, 3, 3)).T
    to_right[...] = sent[:8]
    to_left[...] = sent[8:16]
    near_first, near_last = d_powers(MARGIN), d_powers(MARGIN, -1.0)
    first[...] = jnp.zeros_like(first)
    last[...] = jnp.zeros_like(last)
    for k, source in enumerate((model, inside)):
        lanes = pl.ds(128 * k, 128)
        for i in range(3):
            low, high = source[i, pl.ds(0, MARGIN), :], source[i, pl.ds(ROWS - MARGIN, MARGIN), :]
            first[i : i + 1, lanes] = low[:1]
            last[i : i + 1, lanes] = high[MARGIN - 1 :]
            first[i + 3 : i + 4, lanes] = jnp.sum(near_first * low, axis=0, keepdims=True)
            last[i + 3 : i + 4, lanes] = jnp.sum(near_last * high, axis=0, keepdims=True)
    cross, square = jnp.sum(total[0]), jnp.sum(total[1])
    lane = lax.broadcasted_iota(jnp.int32, sums.shape, 1)
    sums[...] = jnp.where(lane < 64, cross, square)


def local_kernel(edge, inside, xt, yt, edge_out, inside_out, held):
    none = jnp.zeros((MARGIN, COLS), F32)

    def model(i, start, length):
        rows = pl.ds(start, length)
        return jnp.concatenate([edge[i, rows, :], inside[i, rows, :]], axis=1)

    for c, (i, j) in enumerate(((0, 1), (1, 3), (2, 4))):
        high, low = parts(model(j, 0, ROWS))
        along_y = dot(jnp.concatenate([high, low, high], axis=1), thrice(yt))
        for start in range(0, ROWS, TILE):
            tile = min(TILE, ROWS - start)
            rows = pl.ds(start, tile)
            begin, end = max(start - MARGIN, 0), min(start + TILE + MARGIN, ROWS)
            window = model(i, begin, end - begin)
            if begin == 0:
                window = jnp.concatenate([none, window], axis=0)
            if window.shape[0] < WINDOW:
                window = jnp.concatenate([window, jnp.zeros((WINDOW - window.shape[0], COLS), F32)], axis=0)
            high, low = parts(window)
            a, b = dot(xt[...], high), dot(xt[pl.ds(0, TILE), :], low)
            both = (a[:tile] + (a[TILE : TILE + tile] + b[:tile])) + along_y[start : start + tile]
            if c == 0:
                held[rows, :] = both
            else:
                edge_out[j, rows, :], inside_out[j, rows, :] = both[:, :128], both[:, 128:]
    edge_out[0], inside_out[0] = held[:, pl.ds(0, 128)], held[:, pl.ds(128, 128)]


def halo_kernel(edge, inside, before, after, left, right, ht, edge_out, inside_out):
    halo = jnp.concatenate([left[...], right[...], jnp.zeros((112, ROWS), F32)], axis=0)
    high, low = parts(halo.T)
    high, low = high[:, :16], low[:, :16]
    added = dot(jnp.concatenate([high, low, high], axis=1), thrice(ht))
    row = lax.broadcasted_iota(jnp.int32, (MARGIN, 1), 0)
    for c, i in enumerate((0, 3, 4)):
        edge_out[i] = edge[i] + added[:, c * 128 : (c + 1) * 128]
        inside_out[i] = inside[i]
        for strip, sign, start in ((before, 1.0, 0), (after, -1.0, ROWS - MARGIN)):
            decay = d_powers(MARGIN, sign) * float(sign * D_FAR / POLE_D)
            near = jnp.where(row == (0 if start == 0 else MARGIN - 1), sign * D_NEAR * strip[c : c + 1], 0.0)
            part = decay * strip[c + 3 : c + 4] + near
            rows = pl.ds(start, MARGIN)
            edge_out[i, rows, :] += part[:, :128]
            inside_out[i, rows, :] += part[:, 128:]


def scale_kernel(edge, inside, sums, out, coefficient, held, sems):
    groups = coefficient.shape[0]
    part = sums[...]
    plane = lax.broadcasted_iota(jnp.int32, part.shape, 0) % groups
    at = lax.axis_index("gz")
    scale = jnp.zeros((1, 1), F32)
    ratios = []
    for g in range(groups):
        mean = jnp.sum(jnp.where(plane == g, part, 0.0), axis=0, keepdims=True) * (
            groups / (part.shape[0] * ROWS * COLS)
        )
        ratios.append(mean[:, 0:1] / (mean[:, 64:65] + 1e-06))
        scale = jnp.where(at == g, ratios[g], scale)
    copies = []
    half = ROWS // 2
    outer = lax.broadcasted_iota(jnp.int32, (half, 128), 1) < 64
    for t in range(2):
        rows = pl.ds(t * half, half)
        for c, i in enumerate((0, 3, 4)):
            e, m = scale * edge[i, rows, :], scale * inside[i, rows, :]
            held[c, rows, pl.ds(0, 128)] = jnp.where(outer, e, m)
            held[c, rows, pl.ds(128, 128)] = jnp.where(outer, m, e)
            copy = pltpu.make_async_copy(held.at[c, rows, :], out.at[c, rows, :], sems.at[t, c])
            copy.start()
            copies.append(copy)
    for g in range(groups):
        coefficient[g] = ratios[g][0, 0]
    for copy in copies:
        copy.wait()


VMEM = pl.BlockSpec(memory_space=pltpu.VMEM)


def call(kernel, outs, flops, limit, *args, scratch=(), out_specs=None, aliases=None):
    return pl.pallas_call(
        kernel,
        out_shape=[jax.ShapeDtypeStruct(s, d) for s, d in outs],
        in_specs=[VMEM] * len(args),
        out_specs=out_specs or [VMEM] * len(outs),
        scratch_shapes=list(scratch),
        input_output_aliases=aliases or {},
        cost_estimate=pl.CostEstimate(flops=int(flops), bytes_accessed=6 << 20, transcendentals=0),
        compiler_params=pltpu.CompilerParams(vmem_limit_bytes=limit << 20),
    )(*args)


def exchange(to_next, to_previous, axis):
    n = lax.axis_size(axis)
    up = [(i, (i + 1) % n) for i in range(n)]
    down = [(j, i) for i, j in up]
    return lax.ppermute(to_next, axis, up), lax.ppermute(to_previous, axis, down)


def on_device(velocity):
    v = velocity[:, 0]
    edge = jnp.asarray(edge_tables())
    strip = ((3, MARGIN, COLS), F32)
    first, last = call(strip_kernel, [strip, strip], 2e11, 2, v[:, :MARGIN], v[:, ROWS - MARGIN :])
    before, after = exchange(last, first, "gx")
    middle, sent = call(
        middle_kernel,
        [((12, 2, INNER, COLS), BF), ((INNER, 128), F32)],
        4e9, 10,
        v, jnp.asarray(x_tables(TILE)), jnp.asarray(x_tables(INNER % TILE)), edge,
        scratch=[pltpu.VMEM((INNER, 1792), BF)],
    )
    outer, to_right, to_left = call(
        outer_kernel,
        [((12, 2, 2 * MARGIN, COLS), BF), ((SENT_PAD, ROWS), F32), ((SENT_PAD, ROWS), F32)],
        1e9, 8,
        v, before, after, sent, jnp.asarray(x_tables(MARGIN)), edge,
        scratch=[pltpu.VMEM((2 * MARGIN, 1792), BF)],
    )
    left, right = exchange(to_right, to_left, "gy")
    half = ((5, ROWS, 128), F32)
    local, inside, inside_sums = call(
        y_kernel,
        [((15, ROWS, 128), F32), half, ((2, CHUNK, 128), F32)],
        4e9, 12,
        middle, outer, jnp.asarray(y_tables()),
        scratch=[pltpu.VMEM((15, ROWS, 128), F32)],
    )
    devices = lax.axis_size("gx") * lax.axis_size("gy") * lax.axis_size("gz")
    model, first, last, to_right, to_left, sums = call(
        model_kernel,
        [
            half,
            ((8, COLS), F32),
            ((8, COLS), F32),
            ((8, ROWS), F32),
            ((8, ROWS), F32),
            ((devices, 128), F32),
        ],
        4e9, 12,
        local, inside, inside_sums, left, right, jnp.asarray(halo_tables()), jnp.asarray(d_edge_tables()),
        scratch=[
            pltpu.VMEM((256, ROWS), F32),
            pltpu.VMEM((ROWS, 15 * 128), F32),
            pltpu.VMEM((2, CHUNK, 128), F32),
        ],
    )
    sums = lax.all_to_all(sums, ("gx", "gy", "gz"), 0, 0, tiled=True)
    before, after = exchange(last, first, "gx")
    left, right = exchange(to_right, to_left, "gy")
    model, inside = call(
        local_kernel,
        [half, half],
        4e9, 8,
        model, inside, jnp.asarray(d_x_tables()), jnp.asarray(d_y_tables()),
        scratch=[pltpu.VMEM((ROWS, COLS), F32)],
        aliases={0: 0, 1: 1},
    )
    field = ((3, ROWS, COLS), F32)
    model, inside = call(
        halo_kernel,
        [half, half],
        1e9, 8,
        model, inside, before, after, left, right, jnp.asarray(d_halo_tables()),
        aliases={0: 0, 1: 1},
    )
    divergence, coefficient = call(
        scale_kernel,
        [field, ((lax.axis_size("gz"),), F32)],
        1e8, 8,
        model, inside, sums,
        out_specs=[pl.BlockSpec(memory_space=pltpu.HBM), pl.BlockSpec(memory_space=pltpu.SMEM)],
        scratch=[pltpu.VMEM((3, ROWS, COLS), F32), pltpu.SemaphoreType.DMA((2, 3))],
    )
    return divergence[:, None], coefficient


def solution(mesh):
    return jax.shard_map(
        on_device,
        mesh=mesh,
        in_specs=(P(None, "gz", "gx", "gy"),),
        out_specs=(P(None, "gz", "gx", "gy"), P()),
        check_vma=False,
    )
```

profile of v0, /device:TPU:1, one launch (start us, length us, event | category | flops | bytes accessed | tf_op | source)
XLA Modules:
  0.0 49.7 jit_solution(3065997200992421148)
XLA Ops:
  0.6 1.0 %fusion = (f32[3,32,256]{2,1,0:T(8,128)S(1)}, f32[3,32,256]{2,1,0:T(8,128)S(1)}) fusion(f32[3,512,256]{2,1,0:T(8,128)} %bitcast.9), kind=kLoop, calls=%fused_computation | loop fusion | bytes 393216 | tf_op jit(solution)/shard_map/slice | solution.py:473
  1.6 0.0 copy-start
  1.6 0.0 copy-start.3
  1.6 0.0 copy-start.5
  1.6 0.0 copy-start.8
  1.7 2.6 %collective-permute-start = (f32[3,32,256]{2,1,0:T(8,128)S(1)}, f32[3,32,256]{2,1,0:T(8,128)S(1)}, u32[]{:S(2)}, u32[]{:S(2)}) collective-permute-start(f32[3,32,256]{2,1,0:T(8,128)S(1)} %get-tuple-element.25), channel_id=1, source_target_pairs={{0,32},{32,64},{64,96},{96,128},{128,160},{160,192},{192,224},{224... | collective-permute-start | bytes 294920 | tf_op jit(solution)/shard_map/ppermute | solution.py:466
  4.3 0.7 %collective-permute-start.1 = (f32[3,32,256]{2,1,0:T(8,128)S(1)}, f32[3,32,256]{2,1,0:T(8,128)S(1)}, u32[]{:S(2)}, u32[]{:S(2)}) collective-permute-start(f32[3,32,256]{2,1,0:T(8,128)S(1)} %get-tuple-element.26), channel_id=1, source_target_pairs={{32,0},{64,32},{96,64},{128,96},{160,128},{192,160},{224,192},{0,2... | collective-permute-start | bytes 294920 | tf_op jit(solution)/shard_map/ppermute | solution.py:466
  5.0 3.1 %shard_map.122 = (bf16[12,2,448,256]{3,2,1,0:T(8,128)(2,1)S(1)}, f32[448,128]{1,0:T(8,128)S(1)}) custom-call(f32[3,512,256]{2,1,0:T(8,128)S(1)} %bitcast.10, bf16[256,576]{1,0:T(8,128)(2,1)S(1)} %copy-done.3, bf16[128,384]{1,0:T(8,128)(2,1)S(1)} %copy-done.8, bf16[1024,128]{1,0:T(8,128)(2,1)S(1)} %copy-done.5), custom_call_target="tpu_custom_call" | custom-call | flops 4000000000 | bytes 6291456 | tf_op jit(solution)/shard_map/pallas_call | solution.py:450
  8.1 0.0 collective-permute-done.before
  8.1 0.2 collective-permute-done.1.after
  8.3 0.9 %shard_map.124 = (bf16[12,2,64,256]{3,2,1,0:T(8,128)(2,1)S(1)}, f32[48,512]{1,0:T(8,128)S(1)}, f32[48,512]{1,0:T(8,128)S(1)}) custom-call(f32[3,512,256]{2,1,0:T(8,128)S(1)} %bitcast.11, f32[3,32,256]{2,1,0:T(8,128)S(1)} %collective-permute-done.before, f32[3,32,256]{2,1,0:T(8,128)S(1)} %collective-permute-done.1.after, ...), custom_call_target="tpu_custom_call" | custom-call | flops 1000000000 | bytes 6291456 | tf_op jit(solution)/shard_map/pallas_call | solution.py:450
  9.2 1.4 %collective-permute-start.2 = (f32[48,512]{1,0:T(8,128)S(1)}, f32[48,512]{1,0:T(8,128)S(1)}, u32[]{:S(2)}, u32[]{:S(2)}) collective-permute-start(f32[48,512]{1,0:T(8,128)S(1)} %get-tuple-element.32), channel_id=1, source_target_pairs={{0,2},{2,4},{4,6},{6,8},{8,10},{10,12},{12,14},{14,16},{16,18},{18... | collective-permute-start | bytes 294920 | tf_op jit(solution)/shard_map/ppermute | solution.py:466
  10.6 5.4 %collective-permute-start.3 = (f32[48,512]{1,0:T(8,128)S(1)}, f32[48,512]{1,0:T(8,128)S(1)}, u32[]{:S(2)}, u32[]{:S(2)}) collective-permute-start(f32[48,512]{1,0:T(8,128)S(1)} %get-tuple-element.33), channel_id=1, source_target_pairs={{2,0},{4,2},{6,4},{8,6},{10,8},{12,10},{14,12},{16,14},{18,16},{20... | collective-permute-start | bytes 294920 | tf_op jit(solution)/shard_map/ppermute | solution.py:466
  16.0 3.8 %shard_map.125 = (f32[15,512,128]{2,1,0:T(8,128)S(1)}, f32[5,512,128]{2,1,0:T(8,128)S(1)}, f32[2,16,128]{2,1,0:T(8,128)S(1)}) custom-call(bf16[12,2,448,256]{3,2,1,0:T(8,128)(2,1)S(1)} %get-tuple-element.24.middle, bf16[12,2,64,256]{3,2,1,0:T(8,128)(2,1)S(1)} %get-tuple-element.28.outer, bf16[512,512]{1,0:T(8,128)(2,1)S(1)} %copy-done.2), custom_call_target="tpu_custom_call" | custom-call | flops 4000000000 | bytes 6291456 | tf_op jit(solution)/shard_map/pallas_call | solution.py:450
  19.8 0.0 collective-permute-done.2.left
  19.8 0.0 collective-permute-done.3.right
  19.9 0.0 copy-start.4
  19.9 0.0 copy-start.7
  19.9 3.1 %shard_map.126 = (f32[5,512,128]{2,1,0:T(8,128)S(1)}, f32[8,256]{1,0:T(8,128)S(1)}, f32[8,256]{1,0:T(8,128)S(1)}, f32[8,512]{1,0:T(8,128)S(1)}, f32[8,512]{1,0:T(8,128)S(1)}, /*index=5*/f32[256,128]{1,0:T(8,128)}) custom-call(f32[15,512,128]{2,1,0:T(8,128)S(1)} %get-tuple-element.29.local, f32[5,512,128]{2,1,0:T(8,128)S(1)} %get-tuple-element.30.inside, ...), custom_call_target="tpu_custom_call" | custom-call | flops 4000000000 | bytes 6291456 | tf_op jit(solution)/shard_map/pallas_call | solution.py:450
  23.0 11.8 %all-to-all-start = ((f32[256,1,128]{2,1,0:T(1,128)}), f32[256,1,128]{2,1,0:T(1,128)S(1)}, u32[]{:S(2)}, u32[]{:S(2)}) async-start(f32[256,1,128]{2,1,0:T(1,128)} %bitcast.2), calls=%async_computation | async-start | bytes 262144 | tf_op jit(solution)/shard_map/all_to_all | solution.py:517
  34.9 1.6 %collective-permute-start.4 = (f32[8,256]{1,0:T(8,128)S(1)}, f32[8,256]{1,0:T(8,128)S(1)}, u32[]{:S(2)}, u32[]{:S(2)}) collective-permute-start(f32[8,256]{1,0:T(8,128)S(1)} %get-tuple-element.37), channel_id=1, source_target_pairs={{0,32},{32,64},{64,96},{96,128},{128,160},{160,192},{192,224},{224... | collective-permute-start | bytes 24584 | tf_op jit(solution)/shard_map/ppermute | solution.py:466
  36.5 0.5 %collective-permute-start.5 = (f32[8,256]{1,0:T(8,128)S(1)}, f32[8,256]{1,0:T(8,128)S(1)}, u32[]{:S(2)}, u32[]{:S(2)}) collective-permute-start(f32[8,256]{1,0:T(8,128)S(1)} %get-tuple-element.38), channel_id=1, source_target_pairs={{32,0},{64,32},{96,64},{128,96},{160,128},{192,160},{224,192},{0,2... | collective-permute-start | bytes 24584 | tf_op jit(solution)/shard_map/ppermute | solution.py:466
  37.0 0.7 %collective-permute-start.6 = (f32[8,512]{1,0:T(8,128)S(1)}, f32[8,512]{1,0:T(8,128)S(1)}, u32[]{:S(2)}, u32[]{:S(2)}) collective-permute-start(f32[8,512]{1,0:T(8,128)S(1)} %get-tuple-element.39), channel_id=1, source_target_pairs={{0,2},{2,4},{4,6},{6,8},{8,10},{10,12},{12,14},{14,16},{16,18},{18... | collective-permute-start | bytes 49160 | tf_op jit(solution)/shard_map/ppermute | solution.py:466
  37.7 3.9 %collective-permute-start.7 = (f32[8,512]{1,0:T(8,128)S(1)}, f32[8,512]{1,0:T(8,128)S(1)}, u32[]{:S(2)}, u32[]{:S(2)}) collective-permute-start(f32[8,512]{1,0:T(8,128)S(1)} %get-tuple-element.40), channel_id=1, source_target_pairs={{2,0},{4,2},{6,4},{8,6},{10,8},{12,10},{14,12},{16,14},{18,16},{20... | collective-permute-start | bytes 49160 | tf_op jit(solution)/shard_map/ppermute | solution.py:466
  41.6 1.4 %shard_map.127 = (f32[5,512,128]{2,1,0:T(8,128)S(1)}, f32[5,512,128]{2,1,0:T(8,128)S(1)}) custom-call(f32[5,512,128]{2,1,0:T(8,128)S(1)} %get-tuple-element.34.edge, f32[5,512,128]{2,1,0:T(8,128)S(1)} %get-tuple-element.30.inside, bf16[256,192]{1,0:T(8,128)(2,1)S(1)} %copy-done.7, ...), custom_call_target="tpu_custom_call", output_to_operand_aliasing={{0}: (0, {}), {1}: (1, {})} | custom-call | flops 4000000000 | bytes 6291456 | tf_op jit(solution)/shard_map/pallas_call | solution.py:450
  43.1 0.0 collective-permute-done.4.before
  43.1 0.0 collective-permute-done.5.after
  43.1 0.0 collective-permute-done.6.left
  43.1 0.0 collective-permute-done.7.right
  43.1 0.7 %shard_map.128 = (f32[5,512,128]{2,1,0:T(8,128)S(1)}, f32[5,512,128]{2,1,0:T(8,128)S(1)}) custom-call(f32[5,512,128]{2,1,0:T(8,128)S(1)} %get-tuple-element.35.edge, f32[5,512,128]{2,1,0:T(8,128)S(1)} %get-tuple-element.36.inside, f32[8,256]{1,0:T(8,128)S(1)} %collective-permute-done.4.before, ...), custom_call_target="tpu_custom_call", output_to_operand_aliasing={{0}: (0, {}), {1}: (1, {})} | custom-call | flops 1000000000 | bytes 6291456 | tf_op jit(solution)/shard_map/pallas_call | solution.py:450
  43.8 4.0 %all-to-all-done = f32[256,1,128]{2,1,0:T(1,128)S(1)} async-done(((f32[256,1,128]{2,1,0:T(1,128)}), f32[256,1,128]{2,1,0:T(1,128)S(1)}, u32[]{:S(2)}, u32[]{:S(2)}) %all-to-all-start) | async-done | bytes 131104 | tf_op jit(solution)/shard_map/all_to_all | solution.py:517
  47.8 1.9 %shard_map.129 = (f32[3,512,256]{2,1,0:T(8,128)}, f32[2]{0:T(128)}) custom-call(f32[5,512,128]{2,1,0:T(8,128)S(1)} %get-tuple-element.41.edge, f32[5,512,128]{2,1,0:T(8,128)S(1)} %get-tuple-element.42.inside, f32[256,128]{1,0:T(8,128)S(1)} %bitcast.8), custom_call_target="tpu_custom_call" | custom-call | flops 100000000 | bytes 6291456 | tf_op jit(solution)/shard_map/pallas_call | solution.py:450
  (17 shorter events, 0.0 us)
Async XLA Ops:
  1.6 3.4 %copy-start = (f32[3,1,512,256]{3,2,1,0:T(8,128)S(1)}, f32[3,1,512,256]{3,2,1,0:T(8,128)}, u32[]{:S(2)}) copy-start(f32[3,1,512,256]{3,2,1,0:T(8,128)} %param.11) | copy-start | bytes 4718596
  1.6 3.4 %copy-start.3 = (bf16[256,576]{1,0:T(8,128)(2,1)S(1)}, bf16[256,576]{1,0:T(8,128)(2,1)}, u32[]{:S(2)}) copy-start(bf16[256,576]{1,0:T(8,128)(2,1)} %constant.21.clone.table) | copy-start | bytes 884740
  1.6 3.3 %copy-start.5 = (bf16[1024,128]{1,0:T(8,128)(2,1)S(1)}, bf16[1024,128]{1,0:T(8,128)(2,1)}, u32[]{:S(2)}) copy-start(bf16[1024,128]{1,0:T(8,128)(2,1)} %constant.20.clone.edge) | copy-start | bytes 786436
  1.6 3.3 %copy-start.8 = (bf16[128,384]{1,0:T(8,128)(2,1)S(1)}, bf16[128,384]{1,0:T(8,128)(2,1)}, u32[]{:S(2)}) copy-start(bf16[128,384]{1,0:T(8,128)(2,1)} %constant.22.clone.small) | copy-start | bytes 294916
  1.7 6.4 %collective-permute-start = (f32[3,32,256]{2,1,0:T(8,128)S(1)}, f32[3,32,256]{2,1,0:T(8,128)S(1)}, u32[]{:S(2)}, u32[]{:S(2)}) collective-permute-start(f32[3,32,256]{2,1,0:T(8,128)S(1)} %get-tuple-element.25), channel_id=1, source_target_pairs={{0,32},{32,64},{64,96},{96,128},{128,160},{160,192},{192,224},{224... | collective-permute-start | bytes 294920 | tf_op jit(solution)/shard_map/ppermute | solution.py:466
  4.3 4.0 %copy-start.9 = (bf16[64,288]{1,0:T(8,128)(2,1)S(1)}, bf16[64,288]{1,0:T(8,128)(2,1)}, u32[]{:S(2)}) copy-start(bf16[64,288]{1,0:T(8,128)(2,1)} %constant.23.clone.table) | copy-start | bytes 110596
  4.3 4.0 %collective-permute-start.1 = (f32[3,32,256]{2,1,0:T(8,128)S(1)}, f32[3,32,256]{2,1,0:T(8,128)S(1)}, u32[]{:S(2)}, u32[]{:S(2)}) collective-permute-start(f32[3,32,256]{2,1,0:T(8,128)S(1)} %get-tuple-element.26), channel_id=1, source_target_pairs={{32,0},{64,32},{96,64},{128,96},{160,128},{192,160},{224,192},{0,2... | collective-permute-start | bytes 294920 | tf_op jit(solution)/shard_map/ppermute | solution.py:466
  8.3 7.7 %copy-start.2 = (bf16[512,512]{1,0:T(8,128)(2,1)S(1)}, bf16[512,512]{1,0:T(8,128)(2,1)}, u32[]{:S(2)}) copy-start(bf16[512,512]{1,0:T(8,128)(2,1)} %constant.24.clone.table) | copy-start | bytes 1572868
  9.2 10.6 %collective-permute-start.2 = (f32[48,512]{1,0:T(8,128)S(1)}, f32[48,512]{1,0:T(8,128)S(1)}, u32[]{:S(2)}, u32[]{:S(2)}) collective-permute-start(f32[48,512]{1,0:T(8,128)S(1)} %get-tuple-element.32), channel_id=1, source_target_pairs={{0,2},{2,4},{4,6},{6,8},{8,10},{10,12},{12,14},{14,16},{16,18},{18... | collective-permute-start | bytes 294920 | tf_op jit(solution)/shard_map/ppermute | solution.py:466
  10.6 9.2 %collective-permute-start.3 = (f32[48,512]{1,0:T(8,128)S(1)}, f32[48,512]{1,0:T(8,128)S(1)}, u32[]{:S(2)}, u32[]{:S(2)}) collective-permute-start(f32[48,512]{1,0:T(8,128)S(1)} %get-tuple-element.33), channel_id=1, source_target_pairs={{2,0},{4,2},{6,4},{8,6},{10,8},{12,10},{14,12},{16,14},{18,16},{20... | collective-permute-start | bytes 294920 | tf_op jit(solution)/shard_map/ppermute | solution.py:466
  16.0 3.8 %copy-start.1 = (bf16[256,1920]{1,0:T(8,128)(2,1)S(1)}, bf16[256,1920]{1,0:T(8,128)(2,1)}, u32[]{:S(2)}) copy-start(bf16[256,1920]{1,0:T(8,128)(2,1)} %constant.25.clone.table) | copy-start | bytes 2949124
  16.0 3.9 %copy-start.6 = (bf16[768,128]{1,0:T(8,128)(2,1)S(1)}, bf16[768,128]{1,0:T(8,128)(2,1)}, u32[]{:S(2)}) copy-start(bf16[768,128]{1,0:T(8,128)(2,1)} %constant.26.clone.edge) | copy-start | bytes 589828
  19.9 21.8 %copy-start.4 = (bf16[512,256]{1,0:T(8,128)(2,1)S(1)}, bf16[512,256]{1,0:T(8,128)(2,1)}, u32[]{:S(2)}) copy-start(bf16[512,256]{1,0:T(8,128)(2,1)} %constant.28.clone.yt) | copy-start | bytes 786436
  19.9 21.8 %copy-start.7 = (bf16[256,192]{1,0:T(8,128)(2,1)S(1)}, bf16[256,192]{1,0:T(8,128)(2,1)}, u32[]{:S(2)}) copy-start(bf16[256,192]{1,0:T(8,128)(2,1)} %constant.27.clone.xt) | copy-start | bytes 294916
  23.0 24.8 %all-to-all-start = ((f32[256,1,128]{2,1,0:T(1,128)}), f32[256,1,128]{2,1,0:T(1,128)S(1)}, u32[]{:S(2)}, u32[]{:S(2)}) async-start(f32[256,1,128]{2,1,0:T(1,128)} %bitcast.2), calls=%async_computation | async-start | bytes 262144 | tf_op jit(solution)/shard_map/all_to_all | solution.py:517
  34.9 8.2 %collective-permute-start.4 = (f32[8,256]{1,0:T(8,128)S(1)}, f32[8,256]{1,0:T(8,128)S(1)}, u32[]{:S(2)}, u32[]{:S(2)}) collective-permute-start(f32[8,256]{1,0:T(8,128)S(1)} %get-tuple-element.37), channel_id=1, source_target_pairs={{0,32},{32,64},{64,96},{96,128},{128,160},{160,192},{192,224},{224... | collective-permute-start | bytes 24584 | tf_op jit(solution)/shard_map/ppermute | solution.py:466
  36.5 6.6 %collective-permute-start.5 = (f32[8,256]{1,0:T(8,128)S(1)}, f32[8,256]{1,0:T(8,128)S(1)}, u32[]{:S(2)}, u32[]{:S(2)}) collective-permute-start(f32[8,256]{1,0:T(8,128)S(1)} %get-tuple-element.38), channel_id=1, source_target_pairs={{32,0},{64,32},{96,64},{128,96},{160,128},{192,160},{224,192},{0,2... | collective-permute-start | bytes 24584 | tf_op jit(solution)/shard_map/ppermute | solution.py:466
  37.0 6.1 %collective-permute-start.6 = (f32[8,512]{1,0:T(8,128)S(1)}, f32[8,512]{1,0:T(8,128)S(1)}, u32[]{:S(2)}, u32[]{:S(2)}) collective-permute-start(f32[8,512]{1,0:T(8,128)S(1)} %get-tuple-element.39), channel_id=1, source_target_pairs={{0,2},{2,4},{4,6},{6,8},{8,10},{10,12},{12,14},{14,16},{16,18},{18... | collective-permute-start | bytes 49160 | tf_op jit(solution)/shard_map/ppermute | solution.py:466
  37.7 5.4 %collective-permute-start.7 = (f32[8,512]{1,0:T(8,128)S(1)}, f32[8,512]{1,0:T(8,128)S(1)}, u32[]{:S(2)}, u32[]{:S(2)}) collective-permute-start(f32[8,512]{1,0:T(8,128)S(1)} %get-tuple-element.40), channel_id=1, source_target_pairs={{2,0},{4,2},{6,4},{8,6},{10,8},{12,10},{14,12},{16,14},{18,16},{20... | collective-permute-start | bytes 49160 | tf_op jit(solution)/shard_map/ppermute | solution.py:466
  41.6 1.5 %copy-start.10 = (bf16[32,384]{1,0:T(8,128)(2,1)S(1)}, bf16[32,384]{1,0:T(8,128)(2,1)}, u32[]{:S(2)}) copy-start(bf16[32,384]{1,0:T(8,128)(2,1)} %constant.29.clone.ht) | copy-start | bytes 73732
where the time goes:
time: 49.9 us; the launch traced here: 49.7 us
  starting transfers between devices  28.6 us (57%)
  Pallas kernels  15 us (30%)
  waiting for transfers between devices  4.23 us (8%)
  local copies, waits for them, and re-layouts  1.02 us (2%)
  between operations  0.82 us (2%)
    pallas_call x8, Pallas kernels, call(): pl.pallas_call(kernel, out_shape=[jax.ShapeDtypeStruct(s, d) for s, d in...  15 us
    all_to_all x1, starting transfers between devices, on_device(): sums = lax.all_to_all(sums, ('gx', 'gy', 'gz'), 0, 0, tiled=True)  11.8 us
    ppermute x4, starting transfers between devices, exchange(): lax.ppermute(to_previous, axis, down)  10.5 us
    ppermute x4, starting transfers between devices, exchange(): lax.ppermute(to_next, axis, up)  6.28 us
    all_to_all x1, waiting for transfers between devices, on_device(): sums = lax.all_to_all(sums, ('gx', 'gy', 'gz'), 0, 0, tiled=True)  4.01 us
  transfers between devices with their start and end apart: 9, of which 2 were waited for; matrix products, arithmetic and copies ran while one was open for 0% of the time, Pallas kernels for 18%

commit v1 on v0

--- a/solution.py
+++ b/solution.py
@@ -10,6 +10,7 @@
 ROWS = 512
 COLS = 256
 MARGIN = 32
+HALO = 24
 TILE = 128
 WINDOW = TILE + 2 * MARGIN
 INNER = ROWS - 2 * MARGIN
@@ -254,11 +255,13 @@
 
 
 def outer_kernel(v, before, after, middle, table, edge, out, to_right, to_left, mixed):
+    none = jnp.zeros((MARGIN - HALO, COLS), F32)
+
     def first(i):
-        return jnp.concatenate([before[i], v[i, pl.ds(0, 2 * MARGIN), :]], axis=0)
+        return jnp.concatenate([none, before[i], v[i, pl.ds(0, 2 * MARGIN), :]], axis=0)
 
     def last(i):
-        return jnp.concatenate([v[i, pl.ds(ROWS - 2 * MARGIN, 2 * MARGIN), :], after[i]], axis=0)
+        return jnp.concatenate([v[i, pl.ds(ROWS - 2 * MARGIN, 2 * MARGIN), :], after[i], none], axis=0)
 
     for t, window in enumerate((first, last)):
         rows = pl.ds(t * MARGIN, MARGIN)
@@ -321,7 +324,7 @@
 
 
 def model_kernel(
-    local, inside, inside_sums, left, right, table, edge, model, first, last, to_right, to_left, sums, halo, added, total
+    local, inside_sums, left, right, table, model, sums, halo, added, total
 ):
     high, low = parts(left[...])
     high2, low2 = parts(right[...])
@@ -341,6 +344,12 @@
         return carry
 
     lax.fori_loop(0, ROWS // CHUNK, chunk, 0, unroll=4)
+    cross, square = jnp.sum(total[0]), jnp.sum(total[1])
+    lane = lax.broadcasted_iota(jnp.int32, sums.shape, 1)
+    sums[...] = jnp.where(lane < 64, cross, square)
+
+
+def send_kernel(model, inside, edge, first, last, to_right, to_left):
     main, rest = [], []
     for i in (1, 3, 4):
         high, low = parts(model[i])
@@ -360,9 +369,6 @@
             last[i : i + 1, lanes] = high[MARGIN - 1 :]
             first[i + 3 : i + 4, lanes] = jnp.sum(near_first * low, axis=0, keepdims=True)
             last[i + 3 : i + 4, lanes] = jnp.sum(near_last * high, axis=0, keepdims=True)
-    cross, square = jnp.sum(total[0]), jnp.sum(total[1])
-    lane = lax.broadcasted_iota(jnp.int32, sums.shape, 1)
-    sums[...] = jnp.where(lane < 64, cross, square)
 
 
 def local_kernel(edge, inside, xt, yt, edge_out, inside_out, held):
@@ -412,7 +418,7 @@
             inside_out[i, rows, :] += part[:, 128:]
 
 
-def scale_kernel(edge, inside, sums, out, coefficient, held, sems):
+def scale_kernel(edge, inside, sums, out, coefficient):
     groups = coefficient.shape[0]
     part = sums[...]
     plane = lax.broadcasted_iota(jnp.int32, part.shape, 0) % groups
@@ -425,22 +431,13 @@
         )
         ratios.append(mean[:, 0:1] / (mean[:, 64:65] + 1e-06))
         scale = jnp.where(at == g, ratios[g], scale)
-    copies = []
-    half = ROWS // 2
-    outer = lax.broadcasted_iota(jnp.int32, (half, 128), 1) < 64
-    for t in range(2):
-        rows = pl.ds(t * half, half)
-        for c, i in enumerate((0, 3, 4)):
-            e, m = scale * edge[i, rows, :], scale * inside[i, rows, :]
-            held[c, rows, pl.ds(0, 128)] = jnp.where(outer, e, m)
-            held[c, rows, pl.ds(128, 128)] = jnp.where(outer, m, e)
-            copy = pltpu.make_async_copy(held.at[c, rows, :], out.at[c, rows, :], sems.at[t, c])
-            copy.start()
-            copies.append(copy)
+    outer = lax.broadcasted_iota(jnp.int32, (ROWS, 128), 1) < 64
+    for c, i in enumerate((0, 3, 4)):
+        e, m = scale * edge[i], scale * inside[i]
+        out[c, :, pl.ds(0, 128)] = jnp.where(outer, e, m)
+        out[c, :, pl.ds(128, 128)] = jnp.where(outer, m, e)
     for g in range(groups):
         coefficient[g] = ratios[g][0, 0]
-    for copy in copies:
-        copy.wait()
 
 
 VMEM = pl.BlockSpec(memory_space=pltpu.VMEM)
@@ -469,8 +466,8 @@
 def on_device(velocity):
     v = velocity[:, 0]
     edge = jnp.asarray(edge_tables())
-    strip = ((3, MARGIN, COLS), F32)
-    first, last = call(strip_kernel, [strip, strip], 2e11, 2, v[:, :MARGIN], v[:, ROWS - MARGIN :])
+    strip = ((3, HALO, COLS), F32)
+    first, last = call(strip_kernel, [strip, strip], 2e11, 2, v[:, :HALO], v[:, ROWS - HALO :])
     before, after = exchange(last, first, "gx")
     middle, sent = call(
         middle_kernel,
@@ -496,18 +493,11 @@
         scratch=[pltpu.VMEM((15, ROWS, 128), F32)],
     )
     devices = lax.axis_size("gx") * lax.axis_size("gy") * lax.axis_size("gz")
-    model, first, last, to_right, to_left, sums = call(
+    model, sums = call(
         model_kernel,
-        [
-            half,
-            ((8, COLS), F32),
-            ((8, COLS), F32),
-            ((8, ROWS), F32),
-            ((8, ROWS), F32),
-            ((devices, 128), F32),
-        ],
+        [half, ((devices, 128), F32)],
         4e9, 12,
-        local, inside, inside_sums, left, right, jnp.asarray(halo_tables()), jnp.asarray(d_edge_tables()),
+        local, inside_sums, left, right, jnp.asarray(halo_tables()),
         scratch=[
             pltpu.VMEM((256, ROWS), F32),
             pltpu.VMEM((ROWS, 15 * 128), F32),
@@ -515,6 +505,12 @@
         ],
     )
     sums = lax.all_to_all(sums, ("gx", "gy", "gz"), 0, 0, tiled=True)
+    first, last, to_right, to_left = call(
+        send_kernel,
+        [((8, COLS), F32), ((8, COLS), F32), ((8, ROWS), F32), ((8, ROWS), F32)],
+        1e8, 4,
+        model, inside, jnp.asarray(d_edge_tables()),
+    )
     before, after = exchange(last, first, "gx")
     left, right = exchange(to_right, to_left, "gy")
     model, inside = call(
@@ -538,8 +534,7 @@
         [field, ((lax.axis_size("gz"),), F32)],
         1e8, 8,
         model, inside, sums,
-        out_specs=[pl.BlockSpec(memory_space=pltpu.HBM), pl.BlockSpec(memory_space=pltpu.SMEM)],
-        scratch=[pltpu.VMEM((3, ROWS, COLS), F32), pltpu.SemaphoreType.DMA((2, 3))],
+        out_specs=[VMEM, pl.BlockSpec(memory_space=pltpu.SMEM)],
     )
     return divergence[:, None], coefficient
 

time: 49.9 us -> 48.5 us (0.972)
  waiting for transfers between devices: 4.23 us -> 3.39 us
  Pallas kernels: 15 us -> 14.4 us
    all_to_all x1, waiting for transfers between devices: 4.01 us -> 3.37 us  [on_device(): sums = lax.all_to_all(sums, ('gx', 'gy', 'gz'), 0, 0, tiled=True)]
    pallas_call x8 -> x9, Pallas kernels: 15 us -> 14.4 us  [call(): pl.pallas_call(kernel, out_shape=[jax.ShapeDtypeStruct(s, d) for s, d in...]
  transfers between devices with their start and end apart: 9 -> 9, of which waited for: 2 -> 1; matrix products, arithmetic and copies ran while one was open for 0% -> 0% of each run, Pallas kernels for 18% -> 20%
where the time goes in v1:
time: 48.5 us; the launch traced here: 48.3 us
  starting transfers between devices  28.7 us (59%)
  Pallas kernels  14.4 us (30%)
  waiting for transfers between devices  3.39 us (7%)
  local copies, waits for them, and re-layouts  1.01 us (2%)
  between operations  0.85 us (2%)
    pallas_call x9, Pallas kernels, call(): pl.pallas_call(kernel, out_shape=[jax.ShapeDtypeStruct(s, d) for s, d in...  14.4 us
    all_to_all x1, starting transfers between devices, on_device(): sums = lax.all_to_all(sums, ('gx', 'gy', 'gz'), 0, 0, tiled=True)  11.9 us
    ppermute x4, starting transfers between devices, exchange(): lax.ppermute(to_previous, axis, down)  10.6 us
    ppermute x4, starting transfers between devices, exchange(): lax.ppermute(to_next, axis, up)  6.22 us
    all_to_all x1, waiting for transfers between devices, on_device(): sums = lax.all_to_all(sums, ('gx', 'gy', 'gz'), 0, 0, tiled=True)  3.37 us
  transfers between devices with their start and end apart: 9, of which 1 were waited for; matrix products, arithmetic and copies ran while one was open for 0% of the time, Pallas kernels for 20%

profile of v1, /device:TPU:1, one launch (start us, length us, event | category | flops | bytes accessed | tf_op | source)
XLA Modules:
  0.0 48.3 jit_solution(12759859773860917798)
XLA Ops:
  0.6 0.9 %fusion = (f32[3,24,256]{2,1,0:T(8,128)S(1)}, f32[3,24,256]{2,1,0:T(8,128)S(1)}) fusion(f32[3,512,256]{2,1,0:T(8,128)} %bitcast.9), kind=kLoop, calls=%fused_computation | loop fusion | bytes 294912 | tf_op jit(solution)/shard_map/slice | solution.py:470
  1.6 0.0 copy-start.1
  1.6 0.0 copy-start.4
  1.6 0.0 copy-start.6
  1.6 0.0 copy-start.8
  1.6 2.6 %collective-permute-start = (f32[3,24,256]{2,1,0:T(8,128)S(1)}, f32[3,24,256]{2,1,0:T(8,128)S(1)}, u32[]{:S(2)}, u32[]{:S(2)}) collective-permute-start(f32[3,24,256]{2,1,0:T(8,128)S(1)} %get-tuple-element.25), channel_id=1, source_target_pairs={{0,32},{32,64},{64,96},{96,128},{128,160},{160,192},{192,224},{224... | collective-permute-start | bytes 221192 | tf_op jit(solution)/shard_map/ppermute | solution.py:463
  4.3 0.7 %collective-permute-start.1 = (f32[3,24,256]{2,1,0:T(8,128)S(1)}, f32[3,24,256]{2,1,0:T(8,128)S(1)}, u32[]{:S(2)}, u32[]{:S(2)}) collective-permute-start(f32[3,24,256]{2,1,0:T(8,128)S(1)} %get-tuple-element.26), channel_id=1, source_target_pairs={{32,0},{64,32},{96,64},{128,96},{160,128},{192,160},{224,192},{0,2... | collective-permute-start | bytes 221192 | tf_op jit(solution)/shard_map/ppermute | solution.py:463
  4.9 3.1 %shard_map.122 = (bf16[12,2,448,256]{3,2,1,0:T(8,128)(2,1)S(1)}, f32[448,128]{1,0:T(8,128)S(1)}) custom-call(f32[3,512,256]{2,1,0:T(8,128)S(1)} %bitcast.10, bf16[256,576]{1,0:T(8,128)(2,1)S(1)} %copy-done.4, bf16[128,384]{1,0:T(8,128)(2,1)S(1)} %copy-done.8, bf16[1024,128]{1,0:T(8,128)(2,1)S(1)} %copy-done.6), custom_call_target="tpu_custom_call" | custom-call | flops 4000000000 | bytes 6291456 | tf_op jit(solution)/shard_map/pallas_call | solution.py:447
  8.1 0.0 collective-permute-done.before
  8.1 0.0 collective-permute-done.1.after
  8.1 0.0 copy-start.3
  8.1 0.9 %shard_map.124 = (bf16[12,2,64,256]{3,2,1,0:T(8,128)(2,1)S(1)}, f32[48,512]{1,0:T(8,128)S(1)}, f32[48,512]{1,0:T(8,128)S(1)}) custom-call(f32[3,512,256]{2,1,0:T(8,128)S(1)} %bitcast.11, f32[3,24,256]{2,1,0:T(8,128)S(1)} %collective-permute-done.before, f32[3,24,256]{2,1,0:T(8,128)S(1)} %collective-permute-done.1.after, ...), custom_call_target="tpu_custom_call" | custom-call | flops 1000000000 | bytes 6291456 | tf_op jit(solution)/shard_map/pallas_call | solution.py:447
  9.0 1.3 %collective-permute-start.2 = (f32[48,512]{1,0:T(8,128)S(1)}, f32[48,512]{1,0:T(8,128)S(1)}, u32[]{:S(2)}, u32[]{:S(2)}) collective-permute-start(f32[48,512]{1,0:T(8,128)S(1)} %get-tuple-element.31), channel_id=1, source_target_pairs={{0,2},{2,4},{4,6},{6,8},{8,10},{10,12},{12,14},{14,16},{16,18},{18... | collective-permute-start | bytes 294920 | tf_op jit(solution)/shard_map/ppermute | solution.py:463
  10.3 5.4 %collective-permute-start.3 = (f32[48,512]{1,0:T(8,128)S(1)}, f32[48,512]{1,0:T(8,128)S(1)}, u32[]{:S(2)}, u32[]{:S(2)}) collective-permute-start(f32[48,512]{1,0:T(8,128)S(1)} %get-tuple-element.32), channel_id=1, source_target_pairs={{2,0},{4,2},{6,4},{8,6},{10,8},{12,10},{14,12},{16,14},{18,16},{20... | collective-permute-start | bytes 294920 | tf_op jit(solution)/shard_map/ppermute | solution.py:463
  15.7 3.8 %shard_map.125 = (f32[15,512,128]{2,1,0:T(8,128)S(1)}, f32[5,512,128]{2,1,0:T(8,128)S(1)}, f32[2,16,128]{2,1,0:T(8,128)S(1)}) custom-call(bf16[12,2,448,256]{3,2,1,0:T(8,128)(2,1)S(1)} %get-tuple-element.24.middle, bf16[12,2,64,256]{3,2,1,0:T(8,128)(2,1)S(1)} %get-tuple-element.28.outer, bf16[512,512]{1,0:T(8,128)(2,1)S(1)} %copy-done.3), custom_call_target="tpu_custom_call" | custom-call | flops 4000000000 | bytes 6291456 | tf_op jit(solution)/shard_map/pallas_call | solution.py:447
  19.5 0.0 collective-permute-done.2.left
  19.5 0.0 collective-permute-done.3.right
  19.6 0.0 copy-start
  19.6 2.4 %shard_map.126 = (f32[5,512,128]{2,1,0:T(8,128)S(1)}, f32[256,128]{1,0:T(8,128)}) custom-call(f32[15,512,128]{2,1,0:T(8,128)S(1)} %get-tuple-element.29.local, f32[2,16,128]{2,1,0:T(8,128)S(1)} %get-tuple-element.30.inside_sums, f32[48,512]{1,0:T(8,128)S(1)} %collective-permute-done.2.left, f32[48,512]{1,0:T(8,128)S(1)} %collective-permute-done.3.right, ...), custom_call_target="tpu_custom_call" | custom-call | flops 4000000000 | bytes 6291456 | tf_op jit(solution)/shard_map/pallas_call | solution.py:447
  21.9 11.9 %all-to-all-start = ((f32[256,1,128]{2,1,0:T(1,128)}), f32[256,1,128]{2,1,0:T(1,128)S(1)}, u32[]{:S(2)}, u32[]{:S(2)}) async-start(f32[256,1,128]{2,1,0:T(1,128)} %bitcast.2), calls=%async_computation | async-start | bytes 262144 | tf_op jit(solution)/shard_map/all_to_all | solution.py:507
  33.8 0.0 copy-start.5
  33.8 0.0 copy-start.7
  33.8 0.5 %shard_map.128 = (f32[8,256]{1,0:T(8,128)S(1)}, f32[8,256]{1,0:T(8,128)S(1)}, f32[8,512]{1,0:T(8,128)S(1)}, f32[8,512]{1,0:T(8,128)S(1)}) custom-call(f32[5,512,128]{2,1,0:T(8,128)S(1)} %get-tuple-element.33.edge.model, f32[5,512,128]{2,1,0:T(8,128)S(1)} %get-tuple-element.34.inside, bf16[768,128]{1,0:T(8,128)(2,1)S(1)} %copy-done), custom_call_target="tpu_custom_call" | custom-call | flops 100000000 | bytes 6291456 | tf_op jit(solution)/shard_map/pallas_call | solution.py:447
  34.4 1.6 %collective-permute-start.4 = (f32[8,256]{1,0:T(8,128)S(1)}, f32[8,256]{1,0:T(8,128)S(1)}, u32[]{:S(2)}, u32[]{:S(2)}) collective-permute-start(f32[8,256]{1,0:T(8,128)S(1)} %get-tuple-element.37), channel_id=1, source_target_pairs={{0,32},{32,64},{64,96},{96,128},{128,160},{160,192},{192,224},{224... | collective-permute-start | bytes 24584 | tf_op jit(solution)/shard_map/ppermute | solution.py:463
  36.0 0.5 %collective-permute-start.5 = (f32[8,256]{1,0:T(8,128)S(1)}, f32[8,256]{1,0:T(8,128)S(1)}, u32[]{:S(2)}, u32[]{:S(2)}) collective-permute-start(f32[8,256]{1,0:T(8,128)S(1)} %get-tuple-element.38), channel_id=1, source_target_pairs={{32,0},{64,32},{96,64},{128,96},{160,128},{192,160},{224,192},{0,2... | collective-permute-start | bytes 24584 | tf_op jit(solution)/shard_map/ppermute | solution.py:463
  36.5 0.7 %collective-permute-start.6 = (f32[8,512]{1,0:T(8,128)S(1)}, f32[8,512]{1,0:T(8,128)S(1)}, u32[]{:S(2)}, u32[]{:S(2)}) collective-permute-start(f32[8,512]{1,0:T(8,128)S(1)} %get-tuple-element.39), channel_id=1, source_target_pairs={{0,2},{2,4},{4,6},{6,8},{8,10},{10,12},{12,14},{14,16},{16,18},{18... | collective-permute-start | bytes 49160 | tf_op jit(solution)/shard_map/ppermute | solution.py:463
  37.2 4.0 %collective-permute-start.7 = (f32[8,512]{1,0:T(8,128)S(1)}, f32[8,512]{1,0:T(8,128)S(1)}, u32[]{:S(2)}, u32[]{:S(2)}) collective-permute-start(f32[8,512]{1,0:T(8,128)S(1)} %get-tuple-element.40), channel_id=1, source_target_pairs={{2,0},{4,2},{6,4},{8,6},{10,8},{12,10},{14,12},{16,14},{18,16},{20... | collective-permute-start | bytes 49160 | tf_op jit(solution)/shard_map/ppermute | solution.py:463
  41.2 1.4 %shard_map.127 = (f32[5,512,128]{2,1,0:T(8,128)S(1)}, f32[5,512,128]{2,1,0:T(8,128)S(1)}) custom-call(f32[5,512,128]{2,1,0:T(8,128)S(1)} %get-tuple-element.33.edge.model, f32[5,512,128]{2,1,0:T(8,128)S(1)} %get-tuple-element.34.inside, bf16[256,192]{1,0:T(8,128)(2,1)S(1)} %copy-done.7, ...), custom_call_target="tpu_custom_call", output_to_operand_aliasing={{0}: (0, {}), {1}: (1, {})} | custom-call | flops 4000000000 | bytes 6291456 | tf_op jit(solution)/shard_map/pallas_call | solution.py:447
  42.7 0.0 collective-permute-done.5.after
  42.7 0.7 %shard_map.129 = (f32[5,512,128]{2,1,0:T(8,128)S(1)}, f32[5,512,128]{2,1,0:T(8,128)S(1)}) custom-call(f32[5,512,128]{2,1,0:T(8,128)S(1)} %get-tuple-element.35.edge, f32[5,512,128]{2,1,0:T(8,128)S(1)} %get-tuple-element.36.inside, f32[8,256]{1,0:T(8,128)S(1)} %collective-permute-done.4.before, ...), custom_call_target="tpu_custom_call", output_to_operand_aliasing={{0}: (0, {}), {1}: (1, {})} | custom-call | flops 1000000000 | bytes 6291456 | tf_op jit(solution)/shard_map/pallas_call | solution.py:447
  43.4 3.4 %all-to-all-done = f32[256,1,128]{2,1,0:T(1,128)S(1)} async-done(((f32[256,1,128]{2,1,0:T(1,128)}), f32[256,1,128]{2,1,0:T(1,128)S(1)}, u32[]{:S(2)}, u32[]{:S(2)}) %all-to-all-start) | async-done | bytes 131104 | tf_op jit(solution)/shard_map/all_to_all | solution.py:507
  46.8 1.5 %shard_map.130 = (f32[3,512,256]{2,1,0:T(8,128)}, f32[2]{0:T(128)}) custom-call(f32[5,512,128]{2,1,0:T(8,128)S(1)} %get-tuple-element.41.edge, f32[5,512,128]{2,1,0:T(8,128)S(1)} %get-tuple-element.42.inside, f32[256,128]{1,0:T(8,128)S(1)} %bitcast.8), custom_call_target="tpu_custom_call" | custom-call | flops 100000000 | bytes 6291456 | tf_op jit(solution)/shard_map/pallas_call | solution.py:447
  (18 shorter events, 0.0 us)
Async XLA Ops:
  1.6 3.4 %copy-start.1 = (f32[3,1,512,256]{3,2,1,0:T(8,128)S(1)}, f32[3,1,512,256]{3,2,1,0:T(8,128)}, u32[]{:S(2)}) copy-start(f32[3,1,512,256]{3,2,1,0:T(8,128)} %param.11) | copy-start | bytes 4718596
  1.6 3.4 %copy-start.4 = (bf16[256,576]{1,0:T(8,128)(2,1)S(1)}, bf16[256,576]{1,0:T(8,128)(2,1)}, u32[]{:S(2)}) copy-start(bf16[256,576]{1,0:T(8,128)(2,1)} %constant.21.clone.table) | copy-start | bytes 884740
  1.6 3.3 %copy-start.6 = (bf16[1024,128]{1,0:T(8,128)(2,1)S(1)}, bf16[1024,128]{1,0:T(8,128)(2,1)}, u32[]{:S(2)}) copy-start(bf16[1024,128]{1,0:T(8,128)(2,1)} %constant.20.clone.edge) | copy-start | bytes 786436
  1.6 3.3 %copy-start.8 = (bf16[128,384]{1,0:T(8,128)(2,1)S(1)}, bf16[128,384]{1,0:T(8,128)(2,1)}, u32[]{:S(2)}) copy-start(bf16[128,384]{1,0:T(8,128)(2,1)} %constant.22.clone.small) | copy-start | bytes 294916
  1.6 6.4 %collective-permute-start = (f32[3,24,256]{2,1,0:T(8,128)S(1)}, f32[3,24,256]{2,1,0:T(8,128)S(1)}, u32[]{:S(2)}, u32[]{:S(2)}) collective-permute-start(f32[3,24,256]{2,1,0:T(8,128)S(1)} %get-tuple-element.25), channel_id=1, source_target_pairs={{0,32},{32,64},{64,96},{96,128},{128,160},{160,192},{192,224},{224... | collective-permute-start | bytes 221192 | tf_op jit(solution)/shard_map/ppermute | solution.py:463
  4.3 3.9 %copy-start.9 = (bf16[64,288]{1,0:T(8,128)(2,1)S(1)}, bf16[64,288]{1,0:T(8,128)(2,1)}, u32[]{:S(2)}) copy-start(bf16[64,288]{1,0:T(8,128)(2,1)} %constant.23.clone.table) | copy-start | bytes 110596
  4.3 3.8 %collective-permute-start.1 = (f32[3,24,256]{2,1,0:T(8,128)S(1)}, f32[3,24,256]{2,1,0:T(8,128)S(1)}, u32[]{:S(2)}, u32[]{:S(2)}) collective-permute-start(f32[3,24,256]{2,1,0:T(8,128)S(1)} %get-tuple-element.26), channel_id=1, source_target_pairs={{32,0},{64,32},{96,64},{128,96},{160,128},{192,160},{224,192},{0,2... | collective-permute-start | bytes 221192 | tf_op jit(solution)/shard_map/ppermute | solution.py:463
  8.1 7.6 %copy-start.3 = (bf16[512,512]{1,0:T(8,128)(2,1)S(1)}, bf16[512,512]{1,0:T(8,128)(2,1)}, u32[]{:S(2)}) copy-start(bf16[512,512]{1,0:T(8,128)(2,1)} %constant.24.clone.table) | copy-start | bytes 1572868
  9.0 10.5 %collective-permute-start.2 = (f32[48,512]{1,0:T(8,128)S(1)}, f32[48,512]{1,0:T(8,128)S(1)}, u32[]{:S(2)}, u32[]{:S(2)}) collective-permute-start(f32[48,512]{1,0:T(8,128)S(1)} %get-tuple-element.31), channel_id=1, source_target_pairs={{0,2},{2,4},{4,6},{6,8},{8,10},{10,12},{12,14},{14,16},{16,18},{18... | collective-permute-start | bytes 294920 | tf_op jit(solution)/shard_map/ppermute | solution.py:463
  10.3 9.2 %collective-permute-start.3 = (f32[48,512]{1,0:T(8,128)S(1)}, f32[48,512]{1,0:T(8,128)S(1)}, u32[]{:S(2)}, u32[]{:S(2)}) collective-permute-start(f32[48,512]{1,0:T(8,128)S(1)} %get-tuple-element.32), channel_id=1, source_target_pairs={{2,0},{4,2},{6,4},{8,6},{10,8},{12,10},{14,12},{16,14},{18,16},{20... | collective-permute-start | bytes 294920 | tf_op jit(solution)/shard_map/ppermute | solution.py:463
  15.7 3.8 %copy-start.2 = (bf16[256,1920]{1,0:T(8,128)(2,1)S(1)}, bf16[256,1920]{1,0:T(8,128)(2,1)}, u32[]{:S(2)}) copy-start(bf16[256,1920]{1,0:T(8,128)(2,1)} %constant.25.clone.table) | copy-start | bytes 2949124
  19.6 14.2 %copy-start = (bf16[768,128]{1,0:T(8,128)(2,1)S(1)}, bf16[768,128]{1,0:T(8,128)(2,1)}, u32[]{:S(2)}) copy-start(bf16[768,128]{1,0:T(8,128)(2,1)} %constant.26.clone.edge) | copy-start | bytes 589828
  21.9 24.8 %all-to-all-start = ((f32[256,1,128]{2,1,0:T(1,128)}), f32[256,1,128]{2,1,0:T(1,128)S(1)}, u32[]{:S(2)}, u32[]{:S(2)}) async-start(f32[256,1,128]{2,1,0:T(1,128)} %bitcast.2), calls=%async_computation | async-start | bytes 262144 | tf_op jit(solution)/shard_map/all_to_all | solution.py:507
  33.8 7.4 %copy-start.5 = (bf16[512,256]{1,0:T(8,128)(2,1)S(1)}, bf16[512,256]{1,0:T(8,128)(2,1)}, u32[]{:S(2)}) copy-start(bf16[512,256]{1,0:T(8,128)(2,1)} %constant.28.clone.yt) | copy-start | bytes 786436
  33.8 7.4 %copy-start.7 = (bf16[256,192]{1,0:T(8,128)(2,1)S(1)}, bf16[256,192]{1,0:T(8,128)(2,1)}, u32[]{:S(2)}) copy-start(bf16[256,192]{1,0:T(8,128)(2,1)} %constant.27.clone.xt) | copy-start | bytes 294916
  34.4 8.3 %collective-permute-start.4 = (f32[8,256]{1,0:T(8,128)S(1)}, f32[8,256]{1,0:T(8,128)S(1)}, u32[]{:S(2)}, u32[]{:S(2)}) collective-permute-start(f32[8,256]{1,0:T(8,128)S(1)} %get-tuple-element.37), channel_id=1, source_target_pairs={{0,32},{32,64},{64,96},{96,128},{128,160},{160,192},{192,224},{224... | collective-permute-start | bytes 24584 | tf_op jit(solution)/shard_map/ppermute | solution.py:463
  36.0 6.7 %collective-permute-start.5 = (f32[8,256]{1,0:T(8,128)S(1)}, f32[8,256]{1,0:T(8,128)S(1)}, u32[]{:S(2)}, u32[]{:S(2)}) collective-permute-start(f32[8,256]{1,0:T(8,128)S(1)} %get-tuple-element.38), channel_id=1, source_target_pairs={{32,0},{64,32},{96,64},{128,96},{160,128},{192,160},{224,192},{0,2... | collective-permute-start | bytes 24584 | tf_op jit(solution)/shard_map/ppermute | solution.py:463
  36.5 6.2 %collective-permute-start.6 = (f32[8,512]{1,0:T(8,128)S(1)}, f32[8,512]{1,0:T(8,128)S(1)}, u32[]{:S(2)}, u32[]{:S(2)}) collective-permute-start(f32[8,512]{1,0:T(8,128)S(1)} %get-tuple-element.39), channel_id=1, source_target_pairs={{0,2},{2,4},{4,6},{6,8},{8,10},{10,12},{12,14},{14,16},{16,18},{18... | collective-permute-start | bytes 49160 | tf_op jit(solution)/shard_map/ppermute | solution.py:463
  37.2 5.5 %copy-start.10 = (bf16[32,384]{1,0:T(8,128)(2,1)S(1)}, bf16[32,384]{1,0:T(8,128)(2,1)}, u32[]{:S(2)}) copy-start(bf16[32,384]{1,0:T(8,128)(2,1)} %constant.29.clone.ht) | copy-start | bytes 73732
  37.2 5.5 %collective-permute-start.7 = (f32[8,512]{1,0:T(8,128)S(1)}, f32[8,512]{1,0:T(8,128)S(1)}, u32[]{:S(2)}, u32[]{:S(2)}) collective-permute-start(f32[8,512]{1,0:T(8,128)S(1)} %get-tuple-element.40), channel_id=1, source_target_pairs={{2,0},{4,2},{6,4},{8,6},{10,8},{12,10},{14,12},{16,14},{18,16},{20... | collective-permute-start | bytes 49160 | tf_op jit(solution)/shard_map/ppermute | solution.py:463

commit v2 on v1

--- a/solution.py
+++ b/solution.py
@@ -1,3 +1,5 @@
+import functools
+
 import jax
 import jax.numpy as jnp
 import ml_dtypes
@@ -17,13 +19,14 @@
 REACH = 64
 POLE_F = -0.5
 POLE_D = (np.sqrt(5.0) - 3.0) / 2.0
-PAIRS = ((0, 0), (0, 1), (0, 2), (1, 1), (1, 2), (2, 2))
-NEAR = (3, 3, 3) + (2,) * 9
-FAR = (2, 2, 2) + (1,) * 9
+FIELDS = 11
+OUTS = FIELDS + 3
+NEAR = (3, 3, 3) + (2,) * 8
+FAR = (2, 2, 2) + (1,) * 8
 SLOTS = tuple(n + f for n, f in zip(NEAR, FAR))
 START = tuple(int(s) for s in np.concatenate(([0], np.cumsum(SLOTS)[:-1])))
 SENT = sum(SLOTS)
-SENT_PAD = 48
+SENT_PAD = 40
 DSENT = 2
 BF = jnp.bfloat16
 F32 = jnp.float32
@@ -115,10 +118,19 @@
     return left_operand(np.concatenate([f, g], axis=0))
 
 
+def outer_tables():
+    rows = []
+    for kernel in (KG, KF):
+        block = toeplitz(kernel, MARGIN, 3 * MARGIN, MARGIN)
+        rows.append(split(np.kron(np.eye(2), block)))
+    (g_high, g_low), (f_high, f_low) = rows
+    return np.concatenate([g_high, f_high, f_low, g_low], axis=0)
+
+
 def edge_tables():
     main, rest = [], []
-    for i in range(0, 12, 2):
-        a, b = [edge_table(NEAR[k], FAR[k], START[k]) for k in (i, i + 1)]
+    for i in range(0, FIELDS, 2):
+        a, b = [edge_table(NEAR[k], FAR[k], START[k]) if k < FIELDS else np.zeros((128, 128)) for k in (i, i + 1)]
         high, low = split(np.concatenate([a[:32], b[96:], b[:32], a[96:]], axis=0))
         main.append(high)
         if i < 3:
@@ -141,10 +153,10 @@
 
 
 def halo_tables():
-    table = np.zeros((2 * SENT, 15 * 128))
-    for out in range(15):
-        field = out if out < 12 else out - 12
-        if out < 12:
+    table = np.zeros((2 * SENT, OUTS * 128))
+    for out in range(OUTS):
+        field = out if out < FIELDS else out - FIELDS
+        if out < FIELDS:
             left = from_left(KF, (POLE_F,), 2, NEAR[field], FAR[field])
             if FAR[field] == 2:
                 left[NEAR[field] + 1] = 0.0
@@ -156,7 +168,7 @@
         start = START[field]
         table[start : start + SLOTS[field], out * 128 : out * 128 + REACH] = left
         table[SENT + start : SENT + start + SLOTS[field], out * 128 + REACH : (out + 1) * 128] = sign * left[:, ::-1]
-    full = np.zeros((256, 15 * 128), ml_dtypes.bfloat16)
+    full = np.zeros((256, OUTS * 128), ml_dtypes.bfloat16)
     high, low = split(table)
     n = 2 * SENT
     full[:n], full[n : 2 * n], full[2 * n : 3 * n] = high, high, low
@@ -208,25 +220,47 @@
     return jnp.dot(a, b, preferred_element_type=F32)
 
 
-def x_tile(window, tile, table, put, mixed, rows):
-    v = [window(i) for i in range(3)]
-    data = v + [v[a] * v[b] for a, b in PAIRS]
-    done = [None] * 12
+def products_of(v):
+    ww = v[2] * v[2]
+    return [v[0] * v[0] - ww, v[1] * v[1] - ww, v[0] * v[1], v[0] * v[2], v[1] * v[2]]
+
+
+def x_outer(table, high, low, both):
+    tile = 2 * MARGIN
+    if not both:
+        a, b = dot(table[pl.ds(tile, 2 * tile), :], high), dot(table[pl.ds(tile, tile), :], low)
+        return a[:tile] + (a[tile:] + b), None
+    a, b = dot(table[...], high), dot(table[pl.ds(0, 2 * tile), :], low)
+    return a[tile : 2 * tile] + (a[2 * tile : 3 * tile] + b[tile:]), a[:tile] + (a[3 * tile :] + b[:tile])
+
+
+def x_inner(table, high, low, both):
+    tile = table.shape[0] // 2
+    stacked = jnp.concatenate([high, low, high], axis=0)
+    if not both:
+        return dot(table[pl.ds(0, tile), :], stacked), None
+    done = dot(table[...], stacked)
+    return done[:tile], done[tile:]
+
+
+def x_tile(v, tile, apply, put, mixed, rows):
+    data = v + products_of(v)
+    done = [None] * FIELDS
     for i, value in enumerate(data):
         high, low = parts(value)
-        stacked = jnp.concatenate([high, low, high], axis=0)
+        f, g = apply(high, low, i < 3)
         if i < 3:
-            both = dot(table[...], stacked)
-            done[i], done[3 + i] = both[:tile], both[tile:]
+            done[i], done[3 + i] = f, g
         else:
-            done[3 + i] = dot(table[pl.ds(0, tile), :], stacked)
+            done[3 + i] = f
     lane = lax.broadcasted_iota(jnp.int32, (tile, 128), 1)
     edges = []
     for i, value in enumerate(done):
         put(i, *parts(value))
         edges.append(jnp.where(lane < 64, value[:, :128], value[:, 128:]))
-    for i in range(0, 12, 2):
-        both = jnp.where((lane < 32) | (lane >= 96), edges[i], pltpu.roll(edges[i + 1], 64, 1))
+    for i in range(0, FIELDS, 2):
+        between = pltpu.roll(edges[i + 1], 64, 1) if i + 1 < FIELDS else 0.0
+        both = jnp.where((lane < 32) | (lane >= 96), edges[i], between)
         high, low = parts(both)
         mixed[rows, pl.ds(128 * i, 128)] = high
         mixed[rows, pl.ds(128 * i + 128, 128)] = low
@@ -238,7 +272,10 @@
     first_out[...], last_out[...] = first[...], last[...]
 
 
-def middle_kernel(v, table, small, edge, out, sent, mixed):
+WHOLE = INNER // 128 * 128
+
+
+def middle_kernel(v, table, small, edge, out, sent, rest, mixed):
     at = 0
     while at < INNER:
         tile = min(TILE, INNER - at)
@@ -248,40 +285,36 @@
             out[i, 0, rows, :] = high
             out[i, 1, rows, :] = low
 
-        window = lambda i: v[i, pl.ds(at, tile + 2 * MARGIN), :]
-        x_tile(window, tile, table if tile == TILE else small, put, mixed, rows)
+        apply = functools.partial(x_inner, table if tile == TILE else small)
+        x_tile([v[i, pl.ds(at, tile + 2 * MARGIN), :] for i in range(3)], tile, apply, put, mixed, rows)
         at += tile
-    sent[...] = dot(mixed[...], edge_operand(edge, 6, 2))
-
-
-def outer_kernel(v, before, after, middle, table, edge, out, to_right, to_left, mixed):
+    every = dot(mixed[...], edge_operand(edge, 6, 2))
+    sent[...] = every[:WHOLE].T
+    rest[...] = every[WHOLE:]
+
+
+def outer_kernel(v, before, after, middle, rest, table, edge, out, to_right, to_left, mixed):
     none = jnp.zeros((MARGIN - HALO, COLS), F32)
-
-    def first(i):
-        return jnp.concatenate([none, before[i], v[i, pl.ds(0, 2 * MARGIN), :]], axis=0)
-
-    def last(i):
-        return jnp.concatenate([v[i, pl.ds(ROWS - 2 * MARGIN, 2 * MARGIN), :], after[i], none], axis=0)
-
-    for t, window in enumerate((first, last)):
-        rows = pl.ds(t * MARGIN, MARGIN)
-
-        def put(i, high, low):
-            out[i, 0, rows, :] = high
-            out[i, 1, rows, :] = low
-
-        x_tile(window, MARGIN, table, put, mixed, rows)
+    first, last = pl.ds(0, 2 * MARGIN), pl.ds(ROWS - 2 * MARGIN, 2 * MARGIN)
+    values = [jnp.concatenate([none, before[i], v[i, first, :], v[i, last, :], after[i], none], axis=0) for i in range(3)]
+
+    def put(i, high, low):
+        out[i, 0] = high
+        out[i, 1] = low
+
+    x_tile(values, 2 * MARGIN, functools.partial(x_outer, table), put, mixed, pl.ds(0, 2 * MARGIN))
     sent = dot(mixed[...], edge_operand(edge, 6, 2))
-    every = jnp.concatenate([sent[:MARGIN], middle[...], sent[MARGIN:]], axis=0).T
-    to_right[...] = every[:SENT_PAD]
-    to_left[...] = every[64 : 64 + SENT_PAD]
+    end = jnp.concatenate([rest[...], sent], axis=0).T
+    for target, start in ((to_right, 0), (to_left, 64)):
+        target[:, pl.ds(0, WHOLE)] = middle[pl.ds(start, SENT_PAD), :]
+        target[:, pl.ds(WHOLE, ROWS - WHOLE)] = end[start : start + SENT_PAD]
 
 
 CHUNK = 16
 
 
 def stress(f, pair_sums):
-    smooth, gx, products, gy = f[0:3], f[3:6], f[6:12], f[12:15]
+    smooth, gx, products, gy = f[0:3], f[3:6], f[6:11], f[11:14]
     sxx, syy = gx[0], gy[1]
     szz = -(sxx + syy)
     sxy = 0.5 * (gy[0] + gx[1])
@@ -289,18 +322,17 @@
     syz = 0.5 * gy[2]
     inner = sxx * sxx + syy * syy + szz * szz + 2.0 * (sxy * sxy + sxz * sxz + syz * syz)
     magnitude = jnp.sqrt(2.0 * inner)
-    strain = (sxx, sxy, sxz, syy, syz, szz)
-    single, double = [
-        sum((products[p] - smooth[PAIRS[p][0]] * smooth[PAIRS[p][1]]) * strain[p] for p in which)
-        for which in ((0, 3, 5), (1, 2, 4))
-    ]
+    strain = (sxx, sxy, sxz, syy, syz)
+    leonard = [product - own for product, own in zip(products, products_of(smooth))]
+    single = leonard[0] * sxx + leonard[1] * syy
+    double = leonard[2] * sxy + leonard[3] * sxz + leonard[4] * syz
     pair_sums[0] += (single + 2.0 * double) * magnitude
     pair_sums[1] += 2.0 * inner * inner
     return [magnitude * strain[i] for i in range(5)]
 
 
 def y_kernel(middle, outer, table, out, model, pair_sums, held):
-    for i in range(12):
+    for i in range(FIELDS):
         high, low = [
             jnp.concatenate(
                 [outer[i, k, pl.ds(0, MARGIN), :], middle[i, k], outer[i, k, pl.ds(MARGIN, MARGIN), :]], axis=0
@@ -311,12 +343,12 @@
         done = dot(data, thrice(table) if i < 3 else thrice(table, slice(0, COLS)))
         out[i], held[i] = done[:, :128], done[:, 128:COLS]
         if i < 3:
-            out[12 + i], held[12 + i] = done[:, COLS : COLS + 128], done[:, COLS + 128 :]
+            out[FIELDS + i], held[FIELDS + i] = done[:, COLS : COLS + 128], done[:, COLS + 128 :]
     pair_sums[...] = jnp.zeros_like(pair_sums)
 
     def chunk(step, carry):
         rows = pl.ds(pl.multiple_of(step * CHUNK, CHUNK), CHUNK)
-        for i, value in enumerate(stress([held[k, rows, :] for k in range(15)], pair_sums)):
+        for i, value in enumerate(stress([held[k, rows, :] for k in range(OUTS)], pair_sums)):
             model[i, rows, :] = value
         return carry
 
@@ -329,16 +361,19 @@
     high, low = parts(left[...])
     high2, low2 = parts(right[...])
     n = SENT
-    halo[...] = jnp.zeros_like(halo)
+    halo[pl.ds(6 * SENT, 256 - 6 * SENT), :] = jnp.zeros((256 - 6 * SENT, ROWS), F32)
     for k, (a, b) in enumerate(((high, high2), (low, low2), (high, high2))):
         halo[pl.ds(2 * n * k, n), :] = a.astype(F32)[:n]
         halo[pl.ds(2 * n * k + n, n), :] = b.astype(F32)[:n]
     total[...] = inside_sums[...]
-    added[...] = dot(halo[...].T.astype(BF), table[...])
+    done = dot(halo[...].T.astype(BF), table[...])
+    added[pl.ds(MARGIN, INNER), :] = done[:INNER]
+    added[pl.ds(0, MARGIN), :] = done[INNER : INNER + MARGIN]
+    added[pl.ds(MARGIN + INNER, MARGIN), :] = done[INNER + MARGIN :]
 
     def chunk(step, carry):
         rows = pl.ds(pl.multiple_of(step * CHUNK, CHUNK), CHUNK)
-        f = [local[i, rows, :] + added[rows, pl.ds(i * 128, 128)] for i in range(15)]
+        f = [local[i, rows, :] + added[rows, pl.ds(i * 128, 128)] for i in range(OUTS)]
         for i, value in enumerate(stress(f, total)):
             model[i, rows, :] = value
         return carry
@@ -469,28 +504,28 @@
     strip = ((3, HALO, COLS), F32)
     first, last = call(strip_kernel, [strip, strip], 2e11, 2, v[:, :HALO], v[:, ROWS - HALO :])
     before, after = exchange(last, first, "gx")
-    middle, sent = call(
+    middle, sent, rest = call(
         middle_kernel,
-        [((12, 2, INNER, COLS), BF), ((INNER, 128), F32)],
+        [((FIELDS, 2, INNER, COLS), BF), ((128, WHOLE), F32), ((INNER - WHOLE, 128), F32)],
         4e9, 10,
         v, jnp.asarray(x_tables(TILE)), jnp.asarray(x_tables(INNER % TILE)), edge,
         scratch=[pltpu.VMEM((INNER, 1792), BF)],
     )
     outer, to_right, to_left = call(
         outer_kernel,
-        [((12, 2, 2 * MARGIN, COLS), BF), ((SENT_PAD, ROWS), F32), ((SENT_PAD, ROWS), F32)],
+        [((FIELDS, 2, 2 * MARGIN, COLS), BF), ((SENT_PAD, ROWS), F32), ((SENT_PAD, ROWS), F32)],
         1e9, 8,
-        v, before, after, sent, jnp.asarray(x_tables(MARGIN)), edge,
+        v, before, after, sent, rest, jnp.asarray(outer_tables()), edge,
         scratch=[pltpu.VMEM((2 * MARGIN, 1792), BF)],
     )
     left, right = exchange(to_right, to_left, "gy")
     half = ((5, ROWS, 128), F32)
     local, inside, inside_sums = call(
         y_kernel,
-        [((15, ROWS, 128), F32), half, ((2, CHUNK, 128), F32)],
+        [((OUTS, ROWS, 128), F32), half, ((2, CHUNK, 128), F32)],
         4e9, 12,
         middle, outer, jnp.asarray(y_tables()),
-        scratch=[pltpu.VMEM((15, ROWS, 128), F32)],
+        scratch=[pltpu.VMEM((OUTS, ROWS, 128), F32)],
     )
     devices = lax.axis_size("gx") * lax.axis_size("gy") * lax.axis_size("gz")
     model, sums = call(
@@ -500,7 +535,7 @@
         local, inside_sums, left, right, jnp.asarray(halo_tables()),
         scratch=[
             pltpu.VMEM((256, ROWS), F32),
-            pltpu.VMEM((ROWS, 15 * 128), F32),
+            pltpu.VMEM((ROWS, OUTS * 128), F32),
             pltpu.VMEM((2, CHUNK, 128), F32),
         ],
     )

time: 48.5 us -> 47.5 us (0.979)
  Pallas kernels: 14.4 us -> 13.6 us
    pallas_call x9, Pallas kernels: 14.4 us -> 13.6 us  [call(): pl.pallas_call(kernel, out_shape=[jax.ShapeDtypeStruct(s, d) for s, d in...]
  transfers between devices with their start and end apart: 9 -> 9, of which waited for: 1 -> 2; matrix products, arithmetic and copies ran while one was open for 0% -> 0% of each run, Pallas kernels for 20% -> 19%
where the time goes in v2:
time: 47.5 us; the launch traced here: 47.3 us
  starting transfers between devices  28.3 us (60%)
  Pallas kernels  13.6 us (29%)
  waiting for transfers between devices  3.61 us (8%)
  local copies, waits for them, and re-layouts  1 us (2%)
  between operations  0.82 us (2%)
    pallas_call x9, Pallas kernels, call(): pl.pallas_call(kernel, out_shape=[jax.ShapeDtypeStruct(s, d) for s, d in...  13.6 us
    all_to_all x1, starting transfers between devices, on_device(): sums = lax.all_to_all(sums, ('gx', 'gy', 'gz'), 0, 0, tiled=True)  11.4 us
    ppermute x4, starting transfers between devices, exchange(): lax.ppermute(to_previous, axis, down)  10.6 us
    ppermute x4, starting transfers between devices, exchange(): lax.ppermute(to_next, axis, up)  6.31 us
    all_to_all x1, waiting for transfers between devices, on_device(): sums = lax.all_to_all(sums, ('gx', 'gy', 'gz'), 0, 0, tiled=True)  3.37 us
  transfers between devices with their start and end apart: 9, of which 2 were waited for; matrix products, arithmetic and copies ran while one was open for 0% of the time, Pallas kernels for 19%

profile of v2, /device:TPU:1, one launch (start us, length us, event | category | flops | bytes accessed | tf_op | source)
XLA Modules:
  0.0 47.3 jit_solution(12382722597064459390)
XLA Ops:
  0.6 0.9 %fusion = (f32[3,24,256]{2,1,0:T(8,128)S(1)}, f32[3,24,256]{2,1,0:T(8,128)S(1)}) fusion(f32[3,512,256]{2,1,0:T(8,128)} %bitcast.9), kind=kLoop, calls=%fused_computation | loop fusion | bytes 294912 | tf_op jit(solution)/shard_map/slice | solution.py:505
  1.6 0.0 copy-start.1
  1.6 0.0 copy-start.4
  1.6 0.0 copy-start.6
  1.6 0.0 copy-start.9
  1.6 2.6 %collective-permute-start = (f32[3,24,256]{2,1,0:T(8,128)S(1)}, f32[3,24,256]{2,1,0:T(8,128)S(1)}, u32[]{:S(2)}, u32[]{:S(2)}) collective-permute-start(f32[3,24,256]{2,1,0:T(8,128)S(1)} %get-tuple-element.26), channel_id=1, source_target_pairs={{0,32},{32,64},{64,96},{96,128},{128,160},{160,192},{192,224},{224... | collective-permute-start | bytes 221192 | tf_op jit(solution)/shard_map/ppermute | solution.py:498
  4.3 0.7 %collective-permute-start.1 = (f32[3,24,256]{2,1,0:T(8,128)S(1)}, f32[3,24,256]{2,1,0:T(8,128)S(1)}, u32[]{:S(2)}, u32[]{:S(2)}) collective-permute-start(f32[3,24,256]{2,1,0:T(8,128)S(1)} %get-tuple-element.27), channel_id=1, source_target_pairs={{32,0},{64,32},{96,64},{128,96},{160,128},{192,160},{224,192},{0,2... | collective-permute-start | bytes 221192 | tf_op jit(solution)/shard_map/ppermute | solution.py:498
  4.9 2.9 %shard_map.122 = (bf16[11,2,448,256]{3,2,1,0:T(8,128)(2,1)S(1)}, f32[128,384]{1,0:T(8,128)S(1)}, f32[64,128]{1,0:T(8,128)S(1)}) custom-call(f32[3,512,256]{2,1,0:T(8,128)S(1)} %bitcast.10, bf16[256,576]{1,0:T(8,128)(2,1)S(1)} %copy-done.4, bf16[128,384]{1,0:T(8,128)(2,1)S(1)} %copy-done.9, bf16[1024,128]{1,0:T(8,128)(2,1)S(1)} %copy-done.6), custom_call_target="tpu_custom_call" | custom-call | flops 4000000000 | bytes 6291456 | tf_op jit(solution)/shard_map/pallas_call | solution.py:482
  7.8 0.0 collective-permute-done.before
  7.8 0.2 collective-permute-done.1.after
  8.0 0.8 %shard_map.124 = (bf16[11,2,64,256]{3,2,1,0:T(8,128)(2,1)S(1)}, f32[40,512]{1,0:T(8,128)S(1)}, f32[40,512]{1,0:T(8,128)S(1)}) custom-call(f32[3,512,256]{2,1,0:T(8,128)S(1)} %bitcast.11, f32[3,24,256]{2,1,0:T(8,128)S(1)} %collective-permute-done.before, f32[3,24,256]{2,1,0:T(8,128)S(1)} %collective-permute-done.1.after, ...), custom_call_target="tpu_custom_call" | custom-call | flops 1000000000 | bytes 6291456 | tf_op jit(solution)/shard_map/pallas_call | solution.py:482
  8.8 1.4 %collective-permute-start.2 = (f32[40,512]{1,0:T(8,128)S(1)}, f32[40,512]{1,0:T(8,128)S(1)}, u32[]{:S(2)}, u32[]{:S(2)}) collective-permute-start(f32[40,512]{1,0:T(8,128)S(1)} %get-tuple-element.33), channel_id=1, source_target_pairs={{0,2},{2,4},{4,6},{6,8},{8,10},{10,12},{12,14},{14,16},{16,18},{18... | collective-permute-start | bytes 245768 | tf_op jit(solution)/shard_map/ppermute | solution.py:498
  10.2 5.4 %collective-permute-start.3 = (f32[40,512]{1,0:T(8,128)S(1)}, f32[40,512]{1,0:T(8,128)S(1)}, u32[]{:S(2)}, u32[]{:S(2)}) collective-permute-start(f32[40,512]{1,0:T(8,128)S(1)} %get-tuple-element.34), channel_id=1, source_target_pairs={{2,0},{4,2},{6,4},{8,6},{10,8},{12,10},{14,12},{16,14},{18,16},{20... | collective-permute-start | bytes 245768 | tf_op jit(solution)/shard_map/ppermute | solution.py:498
  15.6 3.6 %shard_map.125 = (f32[14,512,128]{2,1,0:T(8,128)S(1)}, f32[5,512,128]{2,1,0:T(8,128)S(1)}, f32[2,16,128]{2,1,0:T(8,128)S(1)}) custom-call(bf16[11,2,448,256]{3,2,1,0:T(8,128)(2,1)S(1)} %get-tuple-element.25.middle, bf16[11,2,64,256]{3,2,1,0:T(8,128)(2,1)S(1)} %get-tuple-element.30.outer, bf16[512,512]{1,0:T(8,128)(2,1)S(1)} %copy-done.3), custom_call_target="tpu_custom_call" | custom-call | flops 4000000000 | bytes 6291456 | tf_op jit(solution)/shard_map/pallas_call | solution.py:482
  19.2 0.0 collective-permute-done.2.left
  19.2 0.0 collective-permute-done.3.right
  19.2 0.0 copy-start
  19.2 2.2 %shard_map.126 = (f32[5,512,128]{2,1,0:T(8,128)S(1)}, f32[256,128]{1,0:T(8,128)}) custom-call(f32[14,512,128]{2,1,0:T(8,128)S(1)} %get-tuple-element.31.local, f32[2,16,128]{2,1,0:T(8,128)S(1)} %get-tuple-element.32.inside_sums, f32[40,512]{1,0:T(8,128)S(1)} %collective-permute-done.2.left, f32[40,512]{1,0:T(8,128)S(1)} %collective-permute-done.3.right, ...), custom_call_target="tpu_custom_call" | custom-call | flops 4000000000 | bytes 6291456 | tf_op jit(solution)/shard_map/pallas_call | solution.py:482
  21.4 11.4 %all-to-all-start = ((f32[256,1,128]{2,1,0:T(1,128)}), f32[256,1,128]{2,1,0:T(1,128)S(1)}, u32[]{:S(2)}, u32[]{:S(2)}) async-start(f32[256,1,128]{2,1,0:T(1,128)} %bitcast.2), calls=%async_computation | async-start | bytes 262144 | tf_op jit(solution)/shard_map/all_to_all | solution.py:542
  32.9 0.0 copy-start.5
  32.9 0.0 copy-start.7
  32.9 0.5 %shard_map.128 = (f32[8,256]{1,0:T(8,128)S(1)}, f32[8,256]{1,0:T(8,128)S(1)}, f32[8,512]{1,0:T(8,128)S(1)}, f32[8,512]{1,0:T(8,128)S(1)}) custom-call(f32[5,512,128]{2,1,0:T(8,128)S(1)} %get-tuple-element.35.edge.model, f32[5,512,128]{2,1,0:T(8,128)S(1)} %get-tuple-element.36.inside, bf16[768,128]{1,0:T(8,128)(2,1)S(1)} %copy-done), custom_call_target="tpu_custom_call" | custom-call | flops 100000000 | bytes 6291456 | tf_op jit(solution)/shard_map/pallas_call | solution.py:482
  33.4 1.6 %collective-permute-start.4 = (f32[8,256]{1,0:T(8,128)S(1)}, f32[8,256]{1,0:T(8,128)S(1)}, u32[]{:S(2)}, u32[]{:S(2)}) collective-permute-start(f32[8,256]{1,0:T(8,128)S(1)} %get-tuple-element.39), channel_id=1, source_target_pairs={{0,32},{32,64},{64,96},{96,128},{128,160},{160,192},{192,224},{224... | collective-permute-start | bytes 24584 | tf_op jit(solution)/shard_map/ppermute | solution.py:498
  35.1 0.5 %collective-permute-start.5 = (f32[8,256]{1,0:T(8,128)S(1)}, f32[8,256]{1,0:T(8,128)S(1)}, u32[]{:S(2)}, u32[]{:S(2)}) collective-permute-start(f32[8,256]{1,0:T(8,128)S(1)} %get-tuple-element.40), channel_id=1, source_target_pairs={{32,0},{64,32},{96,64},{128,96},{160,128},{192,160},{224,192},{0,2... | collective-permute-start | bytes 24584 | tf_op jit(solution)/shard_map/ppermute | solution.py:498
  35.6 0.7 %collective-permute-start.6 = (f32[8,512]{1,0:T(8,128)S(1)}, f32[8,512]{1,0:T(8,128)S(1)}, u32[]{:S(2)}, u32[]{:S(2)}) collective-permute-start(f32[8,512]{1,0:T(8,128)S(1)} %get-tuple-element.41), channel_id=1, source_target_pairs={{0,2},{2,4},{4,6},{6,8},{8,10},{10,12},{12,14},{14,16},{16,18},{18... | collective-permute-start | bytes 49160 | tf_op jit(solution)/shard_map/ppermute | solution.py:498
  36.2 4.0 %collective-permute-start.7 = (f32[8,512]{1,0:T(8,128)S(1)}, f32[8,512]{1,0:T(8,128)S(1)}, u32[]{:S(2)}, u32[]{:S(2)}) collective-permute-start(f32[8,512]{1,0:T(8,128)S(1)} %get-tuple-element.42), channel_id=1, source_target_pairs={{2,0},{4,2},{6,4},{8,6},{10,8},{12,10},{14,12},{16,14},{18,16},{20... | collective-permute-start | bytes 49160 | tf_op jit(solution)/shard_map/ppermute | solution.py:498
  40.3 1.4 %shard_map.127 = (f32[5,512,128]{2,1,0:T(8,128)S(1)}, f32[5,512,128]{2,1,0:T(8,128)S(1)}) custom-call(f32[5,512,128]{2,1,0:T(8,128)S(1)} %get-tuple-element.35.edge.model, f32[5,512,128]{2,1,0:T(8,128)S(1)} %get-tuple-element.36.inside, bf16[256,192]{1,0:T(8,128)(2,1)S(1)} %copy-done.7, ...), custom_call_target="tpu_custom_call", output_to_operand_aliasing={{0}: (0, {}), {1}: (1, {})} | custom-call | flops 4000000000 | bytes 6291456 | tf_op jit(solution)/shard_map/pallas_call | solution.py:482
  41.7 0.0 collective-permute-done.5.after
  41.7 0.0 collective-permute-done.6.left
  41.8 0.7 %shard_map.129 = (f32[5,512,128]{2,1,0:T(8,128)S(1)}, f32[5,512,128]{2,1,0:T(8,128)S(1)}) custom-call(f32[5,512,128]{2,1,0:T(8,128)S(1)} %get-tuple-element.37.edge, f32[5,512,128]{2,1,0:T(8,128)S(1)} %get-tuple-element.38.inside, f32[8,256]{1,0:T(8,128)S(1)} %collective-permute-done.4.before, ...), custom_call_target="tpu_custom_call", output_to_operand_aliasing={{0}: (0, {}), {1}: (1, {})} | custom-call | flops 1000000000 | bytes 6291456 | tf_op jit(solution)/shard_map/pallas_call | solution.py:482
  42.4 3.4 %all-to-all-done = f32[256,1,128]{2,1,0:T(1,128)S(1)} async-done(((f32[256,1,128]{2,1,0:T(1,128)}), f32[256,1,128]{2,1,0:T(1,128)S(1)}, u32[]{:S(2)}, u32[]{:S(2)}) %all-to-all-start) | async-done | bytes 131104 | tf_op jit(solution)/shard_map/all_to_all | solution.py:542
  45.8 1.5 %shard_map.130 = (f32[3,512,256]{2,1,0:T(8,128)}, f32[2]{0:T(128)}) custom-call(f32[5,512,128]{2,1,0:T(8,128)S(1)} %get-tuple-element.43.edge, f32[5,512,128]{2,1,0:T(8,128)S(1)} %get-tuple-element.44.inside, f32[256,128]{1,0:T(8,128)S(1)} %bitcast.8), custom_call_target="tpu_custom_call" | custom-call | flops 100000000 | bytes 6291456 | tf_op jit(solution)/shard_map/pallas_call | solution.py:482
  (18 shorter events, 0.0 us)
Async XLA Ops:
  1.6 3.4 %copy-start.1 = (f32[3,1,512,256]{3,2,1,0:T(8,128)S(1)}, f32[3,1,512,256]{3,2,1,0:T(8,128)}, u32[]{:S(2)}) copy-start(f32[3,1,512,256]{3,2,1,0:T(8,128)} %param.11) | copy-start | bytes 4718596
  1.6 3.4 %copy-start.4 = (bf16[256,576]{1,0:T(8,128)(2,1)S(1)}, bf16[256,576]{1,0:T(8,128)(2,1)}, u32[]{:S(2)}) copy-start(bf16[256,576]{1,0:T(8,128)(2,1)} %constant.21.clone.table) | copy-start | bytes 884740
  1.6 3.3 %copy-start.6 = (bf16[1024,128]{1,0:T(8,128)(2,1)S(1)}, bf16[1024,128]{1,0:T(8,128)(2,1)}, u32[]{:S(2)}) copy-start(bf16[1024,128]{1,0:T(8,128)(2,1)} %constant.20.clone.edge) | copy-start | bytes 786436
  1.6 3.3 %copy-start.9 = (bf16[128,384]{1,0:T(8,128)(2,1)S(1)}, bf16[128,384]{1,0:T(8,128)(2,1)}, u32[]{:S(2)}) copy-start(bf16[128,384]{1,0:T(8,128)(2,1)} %constant.22.clone.small) | copy-start | bytes 294916
  1.6 6.2 %collective-permute-start = (f32[3,24,256]{2,1,0:T(8,128)S(1)}, f32[3,24,256]{2,1,0:T(8,128)S(1)}, u32[]{:S(2)}, u32[]{:S(2)}) collective-permute-start(f32[3,24,256]{2,1,0:T(8,128)S(1)} %get-tuple-element.26), channel_id=1, source_target_pairs={{0,32},{32,64},{64,96},{96,128},{128,160},{160,192},{192,224},{224... | collective-permute-start | bytes 221192 | tf_op jit(solution)/shard_map/ppermute | solution.py:498
  4.3 3.8 %copy-start.8 = (bf16[256,192]{1,0:T(8,128)(2,1)S(1)}, bf16[256,192]{1,0:T(8,128)(2,1)}, u32[]{:S(2)}) copy-start(bf16[256,192]{1,0:T(8,128)(2,1)} %constant.23.clone.table) | copy-start | bytes 294916
  4.3 3.8 %collective-permute-start.1 = (f32[3,24,256]{2,1,0:T(8,128)S(1)}, f32[3,24,256]{2,1,0:T(8,128)S(1)}, u32[]{:S(2)}, u32[]{:S(2)}) collective-permute-start(f32[3,24,256]{2,1,0:T(8,128)S(1)} %get-tuple-element.27), channel_id=1, source_target_pairs={{32,0},{64,32},{96,64},{128,96},{160,128},{192,160},{224,192},{0,2... | collective-permute-start | bytes 221192 | tf_op jit(solution)/shard_map/ppermute | solution.py:498
  8.0 7.5 %copy-start.3 = (bf16[512,512]{1,0:T(8,128)(2,1)S(1)}, bf16[512,512]{1,0:T(8,128)(2,1)}, u32[]{:S(2)}) copy-start(bf16[512,512]{1,0:T(8,128)(2,1)} %constant.24.clone.table) | copy-start | bytes 1572868
  8.8 10.3 %collective-permute-start.2 = (f32[40,512]{1,0:T(8,128)S(1)}, f32[40,512]{1,0:T(8,128)S(1)}, u32[]{:S(2)}, u32[]{:S(2)}) collective-permute-start(f32[40,512]{1,0:T(8,128)S(1)} %get-tuple-element.33), channel_id=1, source_target_pairs={{0,2},{2,4},{4,6},{6,8},{8,10},{10,12},{12,14},{14,16},{16,18},{18... | collective-permute-start | bytes 245768 | tf_op jit(solution)/shard_map/ppermute | solution.py:498
  10.2 9.0 %collective-permute-start.3 = (f32[40,512]{1,0:T(8,128)S(1)}, f32[40,512]{1,0:T(8,128)S(1)}, u32[]{:S(2)}, u32[]{:S(2)}) collective-permute-start(f32[40,512]{1,0:T(8,128)S(1)} %get-tuple-element.34), channel_id=1, source_target_pairs={{2,0},{4,2},{6,4},{8,6},{10,8},{12,10},{14,12},{16,14},{18,16},{20... | collective-permute-start | bytes 245768 | tf_op jit(solution)/shard_map/ppermute | solution.py:498
  15.6 3.6 %copy-start.2 = (bf16[256,1792]{1,0:T(8,128)(2,1)S(1)}, bf16[256,1792]{1,0:T(8,128)(2,1)}, u32[]{:S(2)}) copy-start(bf16[256,1792]{1,0:T(8,128)(2,1)} %constant.25.clone.table) | copy-start | bytes 2752516
  19.2 13.7 %copy-start = (bf16[768,128]{1,0:T(8,128)(2,1)S(1)}, bf16[768,128]{1,0:T(8,128)(2,1)}, u32[]{:S(2)}) copy-start(bf16[768,128]{1,0:T(8,128)(2,1)} %constant.26.clone.edge) | copy-start | bytes 589828
  21.4 24.4 %all-to-all-start = ((f32[256,1,128]{2,1,0:T(1,128)}), f32[256,1,128]{2,1,0:T(1,128)S(1)}, u32[]{:S(2)}, u32[]{:S(2)}) async-start(f32[256,1,128]{2,1,0:T(1,128)} %bitcast.2), calls=%async_computation | async-start | bytes 262144 | tf_op jit(solution)/shard_map/all_to_all | solution.py:542
  32.9 7.4 %copy-start.5 = (bf16[512,256]{1,0:T(8,128)(2,1)S(1)}, bf16[512,256]{1,0:T(8,128)(2,1)}, u32[]{:S(2)}) copy-start(bf16[512,256]{1,0:T(8,128)(2,1)} %constant.28.clone.yt) | copy-start | bytes 786436
  32.9 7.4 %copy-start.7 = (bf16[256,192]{1,0:T(8,128)(2,1)S(1)}, bf16[256,192]{1,0:T(8,128)(2,1)}, u32[]{:S(2)}) copy-start(bf16[256,192]{1,0:T(8,128)(2,1)} %constant.27.clone.xt) | copy-start | bytes 294916
  33.4 8.3 %collective-permute-start.4 = (f32[8,256]{1,0:T(8,128)S(1)}, f32[8,256]{1,0:T(8,128)S(1)}, u32[]{:S(2)}, u32[]{:S(2)}) collective-permute-start(f32[8,256]{1,0:T(8,128)S(1)} %get-tuple-element.39), channel_id=1, source_target_pairs={{0,32},{32,64},{64,96},{96,128},{128,160},{160,192},{192,224},{224... | collective-permute-start | bytes 24584 | tf_op jit(solution)/shard_map/ppermute | solution.py:498
  35.1 6.7 %collective-permute-start.5 = (f32[8,256]{1,0:T(8,128)S(1)}, f32[8,256]{1,0:T(8,128)S(1)}, u32[]{:S(2)}, u32[]{:S(2)}) collective-permute-start(f32[8,256]{1,0:T(8,128)S(1)} %get-tuple-element.40), channel_id=1, source_target_pairs={{32,0},{64,32},{96,64},{128,96},{160,128},{192,160},{224,192},{0,2... | collective-permute-start | bytes 24584 | tf_op jit(solution)/shard_map/ppermute | solution.py:498
  35.6 6.2 %collective-permute-start.6 = (f32[8,512]{1,0:T(8,128)S(1)}, f32[8,512]{1,0:T(8,128)S(1)}, u32[]{:S(2)}, u32[]{:S(2)}) collective-permute-start(f32[8,512]{1,0:T(8,128)S(1)} %get-tuple-element.41), channel_id=1, source_target_pairs={{0,2},{2,4},{4,6},{6,8},{8,10},{10,12},{12,14},{14,16},{16,18},{18... | collective-permute-start | bytes 49160 | tf_op jit(solution)/shard_map/ppermute | solution.py:498
  36.2 5.5 %copy-start.10 = (bf16[32,384]{1,0:T(8,128)(2,1)S(1)}, bf16[32,384]{1,0:T(8,128)(2,1)}, u32[]{:S(2)}) copy-start(bf16[32,384]{1,0:T(8,128)(2,1)} %constant.29.clone.ht) | copy-start | bytes 73732
  36.2 5.5 %collective-permute-start.7 = (f32[8,512]{1,0:T(8,128)S(1)}, f32[8,512]{1,0:T(8,128)S(1)}, u32[]{:S(2)}, u32[]{:S(2)}) collective-permute-start(f32[8,512]{1,0:T(8,128)S(1)} %get-tuple-element.42), channel_id=1, source_target_pairs={{2,0},{4,2},{6,4},{8,6},{10,8},{12,10},{14,12},{16,14},{18,16},{20... | collective-permute-start | bytes 49160 | tf_op jit(solution)/shard_map/ppermute | solution.py:498

commit v3 on v2

--- a/solution.py
+++ b/solution.py
@@ -546,8 +546,8 @@
         1e8, 4,
         model, inside, jnp.asarray(d_edge_tables()),
     )
+    left, right = exchange(to_right, to_left, "gy")
     before, after = exchange(last, first, "gx")
-    left, right = exchange(to_right, to_left, "gy")
     model, inside = call(
         local_kernel,
         [half, half],

time: 47.5 us -> 47.5 us (level)
  no operation moved by 1% of the time
where the time goes in v3:
time: 47.5 us; the launch traced here: 47.3 us
  starting transfers between devices  28.3 us (60%)
  Pallas kernels  13.6 us (29%)
  waiting for transfers between devices  3.61 us (8%)
  local copies, waits for them, and re-layouts  1 us (2%)
  between operations  0.82 us (2%)
    pallas_call x9, Pallas kernels, call(): pl.pallas_call(kernel, out_shape=[jax.ShapeDtypeStruct(s, d) for s, d in...  13.6 us
    all_to_all x1, starting transfers between devices, on_device(): sums = lax.all_to_all(sums, ('gx', 'gy', 'gz'), 0, 0, tiled=True)  11.4 us
    ppermute x4, starting transfers between devices, exchange(): lax.ppermute(to_previous, axis, down)  10.6 us
    ppermute x4, starting transfers between devices, exchange(): lax.ppermute(to_next, axis, up)  6.31 us
    all_to_all x1, waiting for transfers between devices, on_device(): sums = lax.all_to_all(sums, ('gx', 'gy', 'gz'), 0, 0, tiled=True)  3.37 us
  transfers between devices with their start and end apart: 9, of which 2 were waited for; matrix products, arithmetic and copies ran while one was open for 0% of the time, Pallas kernels for 19%

profile of v3, /device:TPU:1, one launch (start us, length us, event | category | flops | bytes accessed | tf_op | source)
XLA Modules:
  0.0 47.3 jit_solution(12382722597064459390)
XLA Ops:
  0.6 0.9 %fusion = (f32[3,24,256]{2,1,0:T(8,128)S(1)}, f32[3,24,256]{2,1,0:T(8,128)S(1)}) fusion(f32[3,512,256]{2,1,0:T(8,128)} %bitcast.9), kind=kLoop, calls=%fused_computation | loop fusion | bytes 294912 | tf_op jit(solution)/shard_map/slice | solution.py:505
  1.6 0.0 copy-start.1
  1.6 0.0 copy-start.4
  1.6 0.0 copy-start.6
  1.6 0.0 copy-start.9
  1.6 2.6 %collective-permute-start = (f32[3,24,256]{2,1,0:T(8,128)S(1)}, f32[3,24,256]{2,1,0:T(8,128)S(1)}, u32[]{:S(2)}, u32[]{:S(2)}) collective-permute-start(f32[3,24,256]{2,1,0:T(8,128)S(1)} %get-tuple-element.26), channel_id=1, source_target_pairs={{0,32},{32,64},{64,96},{96,128},{128,160},{160,192},{192,224},{224... | collective-permute-start | bytes 221192 | tf_op jit(solution)/shard_map/ppermute | solution.py:498
  4.3 0.7 %collective-permute-start.1 = (f32[3,24,256]{2,1,0:T(8,128)S(1)}, f32[3,24,256]{2,1,0:T(8,128)S(1)}, u32[]{:S(2)}, u32[]{:S(2)}) collective-permute-start(f32[3,24,256]{2,1,0:T(8,128)S(1)} %get-tuple-element.27), channel_id=1, source_target_pairs={{32,0},{64,32},{96,64},{128,96},{160,128},{192,160},{224,192},{0,2... | collective-permute-start | bytes 221192 | tf_op jit(solution)/shard_map/ppermute | solution.py:498
  4.9 2.9 %shard_map.122 = (bf16[11,2,448,256]{3,2,1,0:T(8,128)(2,1)S(1)}, f32[128,384]{1,0:T(8,128)S(1)}, f32[64,128]{1,0:T(8,128)S(1)}) custom-call(f32[3,512,256]{2,1,0:T(8,128)S(1)} %bitcast.10, bf16[256,576]{1,0:T(8,128)(2,1)S(1)} %copy-done.4, bf16[128,384]{1,0:T(8,128)(2,1)S(1)} %copy-done.9, bf16[1024,128]{1,0:T(8,128)(2,1)S(1)} %copy-done.6), custom_call_target="tpu_custom_call" | custom-call | flops 4000000000 | bytes 6291456 | tf_op jit(solution)/shard_map/pallas_call | solution.py:482
  7.8 0.0 collective-permute-done.before
  7.8 0.2 collective-permute-done.1.after
  8.0 0.8 %shard_map.124 = (bf16[11,2,64,256]{3,2,1,0:T(8,128)(2,1)S(1)}, f32[40,512]{1,0:T(8,128)S(1)}, f32[40,512]{1,0:T(8,128)S(1)}) custom-call(f32[3,512,256]{2,1,0:T(8,128)S(1)} %bitcast.11, f32[3,24,256]{2,1,0:T(8,128)S(1)} %collective-permute-done.before, f32[3,24,256]{2,1,0:T(8,128)S(1)} %collective-permute-done.1.after, ...), custom_call_target="tpu_custom_call" | custom-call | flops 1000000000 | bytes 6291456 | tf_op jit(solution)/shard_map/pallas_call | solution.py:482
  8.8 1.4 %collective-permute-start.2 = (f32[40,512]{1,0:T(8,128)S(1)}, f32[40,512]{1,0:T(8,128)S(1)}, u32[]{:S(2)}, u32[]{:S(2)}) collective-permute-start(f32[40,512]{1,0:T(8,128)S(1)} %get-tuple-element.33), channel_id=1, source_target_pairs={{0,2},{2,4},{4,6},{6,8},{8,10},{10,12},{12,14},{14,16},{16,18},{18... | collective-permute-start | bytes 245768 | tf_op jit(solution)/shard_map/ppermute | solution.py:498
  10.2 5.4 %collective-permute-start.3 = (f32[40,512]{1,0:T(8,128)S(1)}, f32[40,512]{1,0:T(8,128)S(1)}, u32[]{:S(2)}, u32[]{:S(2)}) collective-permute-start(f32[40,512]{1,0:T(8,128)S(1)} %get-tuple-element.34), channel_id=1, source_target_pairs={{2,0},{4,2},{6,4},{8,6},{10,8},{12,10},{14,12},{16,14},{18,16},{20... | collective-permute-start | bytes 245768 | tf_op jit(solution)/shard_map/ppermute | solution.py:498
  15.6 3.6 %shard_map.125 = (f32[14,512,128]{2,1,0:T(8,128)S(1)}, f32[5,512,128]{2,1,0:T(8,128)S(1)}, f32[2,16,128]{2,1,0:T(8,128)S(1)}) custom-call(bf16[11,2,448,256]{3,2,1,0:T(8,128)(2,1)S(1)} %get-tuple-element.25.middle, bf16[11,2,64,256]{3,2,1,0:T(8,128)(2,1)S(1)} %get-tuple-element.30.outer, bf16[512,512]{1,0:T(8,128)(2,1)S(1)} %copy-done.3), custom_call_target="tpu_custom_call" | custom-call | flops 4000000000 | bytes 6291456 | tf_op jit(solution)/shard_map/pallas_call | solution.py:482
  19.2 0.0 collective-permute-done.2.left
  19.2 0.0 collective-permute-done.3.right
  19.2 0.0 copy-start
  19.2 2.2 %shard_map.126 = (f32[5,512,128]{2,1,0:T(8,128)S(1)}, f32[256,128]{1,0:T(8,128)}) custom-call(f32[14,512,128]{2,1,0:T(8,128)S(1)} %get-tuple-element.31.local, f32[2,16,128]{2,1,0:T(8,128)S(1)} %get-tuple-element.32.inside_sums, f32[40,512]{1,0:T(8,128)S(1)} %collective-permute-done.2.left, f32[40,512]{1,0:T(8,128)S(1)} %collective-permute-done.3.right, ...), custom_call_target="tpu_custom_call" | custom-call | flops 4000000000 | bytes 6291456 | tf_op jit(solution)/shard_map/pallas_call | solution.py:482
  21.4 11.4 %all-to-all-start = ((f32[256,1,128]{2,1,0:T(1,128)}), f32[256,1,128]{2,1,0:T(1,128)S(1)}, u32[]{:S(2)}, u32[]{:S(2)}) async-start(f32[256,1,128]{2,1,0:T(1,128)} %bitcast.2), calls=%async_computation | async-start | bytes 262144 | tf_op jit(solution)/shard_map/all_to_all | solution.py:542
  32.9 0.0 copy-start.5
  32.9 0.0 copy-start.7
  32.9 0.5 %shard_map.128 = (f32[8,256]{1,0:T(8,128)S(1)}, f32[8,256]{1,0:T(8,128)S(1)}, f32[8,512]{1,0:T(8,128)S(1)}, f32[8,512]{1,0:T(8,128)S(1)}) custom-call(f32[5,512,128]{2,1,0:T(8,128)S(1)} %get-tuple-element.35.edge.model, f32[5,512,128]{2,1,0:T(8,128)S(1)} %get-tuple-element.36.inside, bf16[768,128]{1,0:T(8,128)(2,1)S(1)} %copy-done), custom_call_target="tpu_custom_call" | custom-call | flops 100000000 | bytes 6291456 | tf_op jit(solution)/shard_map/pallas_call | solution.py:482
  33.4 1.6 %collective-permute-start.4 = (f32[8,256]{1,0:T(8,128)S(1)}, f32[8,256]{1,0:T(8,128)S(1)}, u32[]{:S(2)}, u32[]{:S(2)}) collective-permute-start(f32[8,256]{1,0:T(8,128)S(1)} %get-tuple-element.39), channel_id=1, source_target_pairs={{0,32},{32,64},{64,96},{96,128},{128,160},{160,192},{192,224},{224... | collective-permute-start | bytes 24584 | tf_op jit(solution)/shard_map/ppermute | solution.py:498
  35.1 0.5 %collective-permute-start.5 = (f32[8,256]{1,0:T(8,128)S(1)}, f32[8,256]{1,0:T(8,128)S(1)}, u32[]{:S(2)}, u32[]{:S(2)}) collective-permute-start(f32[8,256]{1,0:T(8,128)S(1)} %get-tuple-element.40), channel_id=1, source_target_pairs={{32,0},{64,32},{96,64},{128,96},{160,128},{192,160},{224,192},{0,2... | collective-permute-start | bytes 24584 | tf_op jit(solution)/shard_map/ppermute | solution.py:498
  35.6 0.7 %collective-permute-start.6 = (f32[8,512]{1,0:T(8,128)S(1)}, f32[8,512]{1,0:T(8,128)S(1)}, u32[]{:S(2)}, u32[]{:S(2)}) collective-permute-start(f32[8,512]{1,0:T(8,128)S(1)} %get-tuple-element.41), channel_id=1, source_target_pairs={{0,2},{2,4},{4,6},{6,8},{8,10},{10,12},{12,14},{14,16},{16,18},{18... | collective-permute-start | bytes 49160 | tf_op jit(solution)/shard_map/ppermute | solution.py:498
  36.2 4.0 %collective-permute-start.7 = (f32[8,512]{1,0:T(8,128)S(1)}, f32[8,512]{1,0:T(8,128)S(1)}, u32[]{:S(2)}, u32[]{:S(2)}) collective-permute-start(f32[8,512]{1,0:T(8,128)S(1)} %get-tuple-element.42), channel_id=1, source_target_pairs={{2,0},{4,2},{6,4},{8,6},{10,8},{12,10},{14,12},{16,14},{18,16},{20... | collective-permute-start | bytes 49160 | tf_op jit(solution)/shard_map/ppermute | solution.py:498
  40.3 1.4 %shard_map.127 = (f32[5,512,128]{2,1,0:T(8,128)S(1)}, f32[5,512,128]{2,1,0:T(8,128)S(1)}) custom-call(f32[5,512,128]{2,1,0:T(8,128)S(1)} %get-tuple-element.35.edge.model, f32[5,512,128]{2,1,0:T(8,128)S(1)} %get-tuple-element.36.inside, bf16[256,192]{1,0:T(8,128)(2,1)S(1)} %copy-done.7, ...), custom_call_target="tpu_custom_call", output_to_operand_aliasing={{0}: (0, {}), {1}: (1, {})} | custom-call | flops 4000000000 | bytes 6291456 | tf_op jit(solution)/shard_map/pallas_call | solution.py:482
  41.7 0.0 collective-permute-done.5.after
  41.7 0.0 collective-permute-done.6.left
  41.8 0.7 %shard_map.129 = (f32[5,512,128]{2,1,0:T(8,128)S(1)}, f32[5,512,128]{2,1,0:T(8,128)S(1)}) custom-call(f32[5,512,128]{2,1,0:T(8,128)S(1)} %get-tuple-element.37.edge, f32[5,512,128]{2,1,0:T(8,128)S(1)} %get-tuple-element.38.inside, f32[8,256]{1,0:T(8,128)S(1)} %collective-permute-done.4.before, ...), custom_call_target="tpu_custom_call", output_to_operand_aliasing={{0}: (0, {}), {1}: (1, {})} | custom-call | flops 1000000000 | bytes 6291456 | tf_op jit(solution)/shard_map/pallas_call | solution.py:482
  42.4 3.4 %all-to-all-done = f32[256,1,128]{2,1,0:T(1,128)S(1)} async-done(((f32[256,1,128]{2,1,0:T(1,128)}), f32[256,1,128]{2,1,0:T(1,128)S(1)}, u32[]{:S(2)}, u32[]{:S(2)}) %all-to-all-start) | async-done | bytes 131104 | tf_op jit(solution)/shard_map/all_to_all | solution.py:542
  45.8 1.5 %shard_map.130 = (f32[3,512,256]{2,1,0:T(8,128)}, f32[2]{0:T(128)}) custom-call(f32[5,512,128]{2,1,0:T(8,128)S(1)} %get-tuple-element.43.edge, f32[5,512,128]{2,1,0:T(8,128)S(1)} %get-tuple-element.44.inside, f32[256,128]{1,0:T(8,128)S(1)} %bitcast.8), custom_call_target="tpu_custom_call" | custom-call | flops 100000000 | bytes 6291456 | tf_op jit(solution)/shard_map/pallas_call | solution.py:482
  (18 shorter events, 0.0 us)
Async XLA Ops:
  1.6 3.4 %copy-start.1 = (f32[3,1,512,256]{3,2,1,0:T(8,128)S(1)}, f32[3,1,512,256]{3,2,1,0:T(8,128)}, u32[]{:S(2)}) copy-start(f32[3,1,512,256]{3,2,1,0:T(8,128)} %param.11) | copy-start | bytes 4718596
  1.6 3.4 %copy-start.4 = (bf16[256,576]{1,0:T(8,128)(2,1)S(1)}, bf16[256,576]{1,0:T(8,128)(2,1)}, u32[]{:S(2)}) copy-start(bf16[256,576]{1,0:T(8,128)(2,1)} %constant.21.clone.table) | copy-start | bytes 884740
  1.6 3.3 %copy-start.6 = (bf16[1024,128]{1,0:T(8,128)(2,1)S(1)}, bf16[1024,128]{1,0:T(8,128)(2,1)}, u32[]{:S(2)}) copy-start(bf16[1024,128]{1,0:T(8,128)(2,1)} %constant.20.clone.edge) | copy-start | bytes 786436
  1.6 3.3 %copy-start.9 = (bf16[128,384]{1,0:T(8,128)(2,1)S(1)}, bf16[128,384]{1,0:T(8,128)(2,1)}, u32[]{:S(2)}) copy-start(bf16[128,384]{1,0:T(8,128)(2,1)} %constant.22.clone.small) | copy-start | bytes 294916
  1.6 6.2 %collective-permute-start = (f32[3,24,256]{2,1,0:T(8,128)S(1)}, f32[3,24,256]{2,1,0:T(8,128)S(1)}, u32[]{:S(2)}, u32[]{:S(2)}) collective-permute-start(f32[3,24,256]{2,1,0:T(8,128)S(1)} %get-tuple-element.26), channel_id=1, source_target_pairs={{0,32},{32,64},{64,96},{96,128},{128,160},{160,192},{192,224},{224... | collective-permute-start | bytes 221192 | tf_op jit(solution)/shard_map/ppermute | solution.py:498
  4.3 3.8 %copy-start.8 = (bf16[256,192]{1,0:T(8,128)(2,1)S(1)}, bf16[256,192]{1,0:T(8,128)(2,1)}, u32[]{:S(2)}) copy-start(bf16[256,192]{1,0:T(8,128)(2,1)} %constant.23.clone.table) | copy-start | bytes 294916
  4.3 3.8 %collective-permute-start.1 = (f32[3,24,256]{2,1,0:T(8,128)S(1)}, f32[3,24,256]{2,1,0:T(8,128)S(1)}, u32[]{:S(2)}, u32[]{:S(2)}) collective-permute-start(f32[3,24,256]{2,1,0:T(8,128)S(1)} %get-tuple-element.27), channel_id=1, source_target_pairs={{32,0},{64,32},{96,64},{128,96},{160,128},{192,160},{224,192},{0,2... | collective-permute-start | bytes 221192 | tf_op jit(solution)/shard_map/ppermute | solution.py:498
  8.0 7.5 %copy-start.3 = (bf16[512,512]{1,0:T(8,128)(2,1)S(1)}, bf16[512,512]{1,0:T(8,128)(2,1)}, u32[]{:S(2)}) copy-start(bf16[512,512]{1,0:T(8,128)(2,1)} %constant.24.clone.table) | copy-start | bytes 1572868
  8.8 10.3 %collective-permute-start.2 = (f32[40,512]{1,0:T(8,128)S(1)}, f32[40,512]{1,0:T(8,128)S(1)}, u32[]{:S(2)}, u32[]{:S(2)}) collective-permute-start(f32[40,512]{1,0:T(8,128)S(1)} %get-tuple-element.33), channel_id=1, source_target_pairs={{0,2},{2,4},{4,6},{6,8},{8,10},{10,12},{12,14},{14,16},{16,18},{18... | collective-permute-start | bytes 245768 | tf_op jit(solution)/shard_map/ppermute | solution.py:498
  10.2 9.0 %collective-permute-start.3 = (f32[40,512]{1,0:T(8,128)S(1)}, f32[40,512]{1,0:T(8,128)S(1)}, u32[]{:S(2)}, u32[]{:S(2)}) collective-permute-start(f32[40,512]{1,0:T(8,128)S(1)} %get-tuple-element.34), channel_id=1, source_target_pairs={{2,0},{4,2},{6,4},{8,6},{10,8},{12,10},{14,12},{16,14},{18,16},{20... | collective-permute-start | bytes 245768 | tf_op jit(solution)/shard_map/ppermute | solution.py:498
  15.6 3.6 %copy-start.2 = (bf16[256,1792]{1,0:T(8,128)(2,1)S(1)}, bf16[256,1792]{1,0:T(8,128)(2,1)}, u32[]{:S(2)}) copy-start(bf16[256,1792]{1,0:T(8,128)(2,1)} %constant.25.clone.table) | copy-start | bytes 2752516
  19.2 13.7 %copy-start = (bf16[768,128]{1,0:T(8,128)(2,1)S(1)}, bf16[768,128]{1,0:T(8,128)(2,1)}, u32[]{:S(2)}) copy-start(bf16[768,128]{1,0:T(8,128)(2,1)} %constant.26.clone.edge) | copy-start | bytes 589828
  21.4 24.4 %all-to-all-start = ((f32[256,1,128]{2,1,0:T(1,128)}), f32[256,1,128]{2,1,0:T(1,128)S(1)}, u32[]{:S(2)}, u32[]{:S(2)}) async-start(f32[256,1,128]{2,1,0:T(1,128)} %bitcast.2), calls=%async_computation | async-start | bytes 262144 | tf_op jit(solution)/shard_map/all_to_all | solution.py:542
  32.9 7.4 %copy-start.5 = (bf16[512,256]{1,0:T(8,128)(2,1)S(1)}, bf16[512,256]{1,0:T(8,128)(2,1)}, u32[]{:S(2)}) copy-start(bf16[512,256]{1,0:T(8,128)(2,1)} %constant.28.clone.yt) | copy-start | bytes 786436
  32.9 7.4 %copy-start.7 = (bf16[256,192]{1,0:T(8,128)(2,1)S(1)}, bf16[256,192]{1,0:T(8,128)(2,1)}, u32[]{:S(2)}) copy-start(bf16[256,192]{1,0:T(8,128)(2,1)} %constant.27.clone.xt) | copy-start | bytes 294916
  33.4 8.3 %collective-permute-start.4 = (f32[8,256]{1,0:T(8,128)S(1)}, f32[8,256]{1,0:T(8,128)S(1)}, u32[]{:S(2)}, u32[]{:S(2)}) collective-permute-start(f32[8,256]{1,0:T(8,128)S(1)} %get-tuple-element.39), channel_id=1, source_target_pairs={{0,32},{32,64},{64,96},{96,128},{128,160},{160,192},{192,224},{224... | collective-permute-start | bytes 24584 | tf_op jit(solution)/shard_map/ppermute | solution.py:498
  35.1 6.7 %collective-permute-start.5 = (f32[8,256]{1,0:T(8,128)S(1)}, f32[8,256]{1,0:T(8,128)S(1)}, u32[]{:S(2)}, u32[]{:S(2)}) collective-permute-start(f32[8,256]{1,0:T(8,128)S(1)} %get-tuple-element.40), channel_id=1, source_target_pairs={{32,0},{64,32},{96,64},{128,96},{160,128},{192,160},{224,192},{0,2... | collective-permute-start | bytes 24584 | tf_op jit(solution)/shard_map/ppermute | solution.py:498
  35.6 6.2 %collective-permute-start.6 = (f32[8,512]{1,0:T(8,128)S(1)}, f32[8,512]{1,0:T(8,128)S(1)}, u32[]{:S(2)}, u32[]{:S(2)}) collective-permute-start(f32[8,512]{1,0:T(8,128)S(1)} %get-tuple-element.41), channel_id=1, source_target_pairs={{0,2},{2,4},{4,6},{6,8},{8,10},{10,12},{12,14},{14,16},{16,18},{18... | collective-permute-start | bytes 49160 | tf_op jit(solution)/shard_map/ppermute | solution.py:498
  36.2 5.5 %copy-start.10 = (bf16[32,384]{1,0:T(8,128)(2,1)S(1)}, bf16[32,384]{1,0:T(8,128)(2,1)}, u32[]{:S(2)}) copy-start(bf16[32,384]{1,0:T(8,128)(2,1)} %constant.29.clone.ht) | copy-start | bytes 73732
  36.2 5.5 %collective-permute-start.7 = (f32[8,512]{1,0:T(8,128)S(1)}, f32[8,512]{1,0:T(8,128)S(1)}, u32[]{:S(2)}, u32[]{:S(2)}) collective-permute-start(f32[8,512]{1,0:T(8,128)S(1)} %get-tuple-element.42), channel_id=1, source_target_pairs={{2,0},{4,2},{6,4},{8,6},{10,8},{12,10},{14,12},{16,14},{18,16},{20... | collective-permute-start | bytes 49160 | tf_op jit(solution)/shard_map/ppermute | solution.py:498
